TPU v7x, 32 devices: a whole 2x2x4 slice. The times are simulated.
32 devices in a mesh: dp: 16 (over z, y, x), tensor: 2 (over core).
Axes of the slice: x: 2, y: 2, z: 4, core: 2. Of those that a mesh axis runs over, the one named last changes fastest.
Arguments:
- tokens: bfloat16 [16, 1024, 576], P('dp', 'tensor'), may hold values from -6 to 6
- segments: int32 [16, 1024], P('dp'), may hold values from 0 to 4, as said below
- cotangent: bfloat16 [16, 1024, 576], P('dp', 'tensor'), may hold values from -6 to 6
- attn_gain: float32 [576], replicated, may hold values from 0.5 to 1.5
- w_query: bfloat16 [576, 576], replicated, may hold values from -0.25 to 0.25
- w_key: bfloat16 [576, 192], replicated, may hold values from -0.25 to 0.25
- w_value: bfloat16 [576, 192], replicated, may hold values from -0.25 to 0.25
- w_out: bfloat16 [576, 576], replicated, may hold values from -1 to 1
- ffn_gain: float32 [576], replicated, may hold values from 0.5 to 1.5
- w_gate: bfloat16 [576, 1536], P(None, 'tensor'), may hold values from -0.25 to 0.25
- w_up: bfloat16 [576, 1536], P(None, 'tensor'), may hold values from -0.25 to 0.25
- w_down: bfloat16 [1536, 576], P('tensor'), may hold values from -0.15625 to 0.15625
Outputs:
- output: bfloat16 [16, 1024, 576], P('dp', 'tensor')
- grad_input: float32 [16, 1024, 576], P('dp', 'tensor')
- grad_attn_gain: float32 [576], replicated
- grad_w_query: float32 [576, 576], replicated
- grad_w_key: float32 [576, 192], replicated
- grad_w_value: float32 [576, 192], replicated
- grad_w_out: float32 [576, 576], replicated
- grad_ffn_gain: float32 [576], replicated
- grad_w_gate: float32 [576, 1536], P(None, 'tensor')
- grad_w_up: float32 [576, 1536], P(None, 'tensor')
- grad_w_down: float32 [1536, 576], P('tensor')
Inputs may be any that keep to these rules, and one draw needn't show every extreme that they name: `segments`: each row holds exactly five documents numbered 0 to 4 in order, starting at document 0 and rising by one at each document start; no document starts at positions 385 to 640, so one document of each row spans them.
All inputs are finite; a program needn't handle non-finite values.
Results may differ from a plain program's by a relative error of at most 0.023.
Values may be sent and summed in bfloat16 or wider, within the bound.
No kernel may reach another device: no remote copies, remote signals or barrier semaphores. Data moves between devices by JAX's collectives and lax.ppermute only.
A program may use at most 128 MiB of HBM per device.

v0:
```python
import jax
import jax.numpy as jnp
from jax import lax
from jax.sharding import PartitionSpec as P

HEADS = 9
KV_HEADS = 3
HEAD_DIM = 64


EPSILON = 1e-05


def rms_norm(values, gain_vec):
    return (
        values * lax.rsqrt(jnp.mean(values * values, axis=-1, keepdims=True) + EPSILON) * gain_vec
    )


def gated(gate_pre, up_pre):
    return jax.nn.silu(gate_pre) * up_pre


def rotate(values, cos_table, sin_table):
    half_dim = values.shape[-1] // 2
    front_part = values[..., :half_dim]
    back_part = values[..., half_dim:]
    return jnp.concatenate(
        [
            front_part * cos_table - back_part * sin_table,
            back_part * cos_table + front_part * sin_table,
        ],
        axis=-1,
    )


def tables(positions):
    half_dim = HEAD_DIM // 2
    inverse = 10000.0 ** (-2.0 * jnp.arange(half_dim).astype(jnp.float32) / HEAD_DIM)
    angles = positions[:, None] * inverse[None, :]
    return (jnp.cos(angles)[:, None, :], jnp.sin(angles)[:, None, :])


def project(left_mat, right_mat):
    return jnp.dot(left_mat, right_mat, preferred_element_type=jnp.float32)


def project_back(left_mat, right_mat):
    return jnp.einsum("rf,df->rd", left_mat, right_mat, preferred_element_type=jnp.float32)


def outer_sum(left_mat, right_mat):
    return jnp.einsum("rd,rf->df", left_mat, right_mat, preferred_element_type=jnp.float32)


def reduce_end(grad_terms):
    shared = lax.psum(
        (grad_terms[0], grad_terms[1], grad_terms[2], grad_terms[3], grad_terms[4], grad_terms[5]),
        ("dp", "tensor"),
    )
    column = lax.psum((grad_terms[6], grad_terms[7], grad_terms[8]), "dp")
    return tuple(shared) + tuple(column)


def per_device(
    tokens,
    segments,
    cotangent,
    attn_gain,
    w_query,
    w_key,
    w_value,
    w_out,
    ffn_gain,
    w_gate,
    w_up,
    w_down,
):
    seq_count, half_len, model_width = tokens.shape
    row_count = seq_count * half_len
    group_size = HEADS // KV_HEADS
    score_scale = HEAD_DIM ** (-0.5)
    offset = lax.axis_index("tensor") * half_len
    query_pos = (offset + jnp.arange(half_len)).astype(jnp.float32)
    key_pos = jnp.arange(segments.shape[1]).astype(jnp.float32)
    cos_table, sin_table = tables(query_pos)
    own_labels = lax.dynamic_slice_in_dim(segments, offset, half_len, 1)
    allowed = (own_labels[:, :, None] == segments[:, None, :]) & (
        query_pos[None, :, None] >= key_pos[None, None, :]
    )

    def attend_group(operands):
        query_grp, key_grp, value_grp = operands
        scores = (
            jnp.einsum("srqd,skd->srqk", query_grp, key_grp, preferred_element_type=jnp.float32)
            * score_scale
        )
        scores = jnp.where(allowed[:, None], scores, -1e30)
        top_score = jnp.max(scores, axis=-1, keepdims=True)
        exp_scores = jnp.exp(scores - top_score)
        row_total = jnp.sum(exp_scores, axis=-1, keepdims=True)
        attn_probs = (exp_scores / row_total).astype(jnp.bfloat16)
        context = jnp.einsum(
            "srqk,skd->srqd", attn_probs, value_grp, preferred_element_type=jnp.float32
        )
        return (context, (top_score + jnp.log(row_total))[..., 0])

    def attend_back(operands):
        query_grp, key_grp, value_grp, grad_grp, log_total = operands
        scores = (
            jnp.einsum("srqd,skd->srqk", query_grp, key_grp, preferred_element_type=jnp.float32)
            * score_scale
        )
        scores = jnp.where(allowed[:, None], scores, -1e30)
        attn_probs = jnp.exp(scores - log_total[..., None])
        grad_probs = jnp.einsum(
            "srqd,skd->srqk", grad_grp, value_grp, preferred_element_type=jnp.float32
        )
        inner_sum = jnp.sum(attn_probs * grad_probs, axis=-1, keepdims=True)
        grad_scores = (attn_probs * (grad_probs - inner_sum)).astype(jnp.bfloat16)
        grad_query = (
            jnp.einsum("srqk,skd->srqd", grad_scores, key_grp, preferred_element_type=jnp.float32)
            * score_scale
        )
        grad_key = (
            jnp.einsum("srqk,srqd->skd", grad_scores, query_grp, preferred_element_type=jnp.float32)
            * score_scale
        )
        grad_value = jnp.einsum(
            "srqk,srqd->skd",
            attn_probs.astype(jnp.bfloat16),
            grad_grp,
            preferred_element_type=jnp.float32,
        )
        return (grad_query, grad_key, grad_value)

    def forward(stream):
        normed = rms_norm(stream, attn_gain).astype(jnp.bfloat16)
        query_pre = project(normed, w_query).reshape(seq_count, half_len, HEADS, HEAD_DIM)
        key_pre = project(normed, w_key).reshape(seq_count, half_len, KV_HEADS, HEAD_DIM)
        query_rot = rotate(query_pre, cos_table, sin_table).astype(jnp.bfloat16)
        key_rot = (
            rotate(key_pre, cos_table, sin_table)
            .astype(jnp.bfloat16)
            .reshape(seq_count, half_len, KV_HEADS * HEAD_DIM)
        )
        value_own = (
            project(normed, w_value)
            .astype(jnp.bfloat16)
            .reshape(seq_count, half_len, KV_HEADS * HEAD_DIM)
        )
        key_all, value_all = (
            lax.all_gather(key_rot, "tensor", axis=1, tiled=True),
            lax.all_gather(value_own, "tensor", axis=1, tiled=True),
        )
        query_grp = query_rot.reshape(
            seq_count, half_len, KV_HEADS, group_size, HEAD_DIM
        ).transpose(2, 0, 3, 1, 4)
        key_grp = key_all.reshape(seq_count, -1, KV_HEADS, HEAD_DIM).transpose(2, 0, 1, 3)
        value_grp = value_all.reshape(seq_count, -1, KV_HEADS, HEAD_DIM).transpose(2, 0, 1, 3)
        contexts, log_total = lax.map(attend_group, (query_grp, key_grp, value_grp))
        context_low = (
            contexts.transpose(1, 3, 0, 2, 4).reshape(row_count, model_width).astype(jnp.bfloat16)
        )
        middle = stream + project(context_low, w_out)
        ffn_in = rms_norm(middle, ffn_gain).astype(jnp.bfloat16)
        ffn_rows = lax.all_gather(ffn_in, "tensor", axis=0, tiled=True)
        gate_pre = project(ffn_rows, w_gate)
        up_pre = project(ffn_rows, w_up)
        product = gated(gate_pre, up_pre).astype(jnp.bfloat16)
        result = middle + lax.psum_scatter(
            project(product, w_down).astype(jnp.bfloat16), "tensor", scatter_dimension=0, tiled=True
        ).astype(jnp.float32)
        saved_state = (
            normed,
            query_grp,
            key_grp,
            value_grp,
            log_total,
            context_low,
            middle,
            ffn_rows,
            gate_pre,
            up_pre,
            product,
        )
        return (result, saved_state)

    def backward(stream, grad_result):
        _, saved_state = forward(stream)
        (
            normed,
            query_grp,
            key_grp,
            value_grp,
            log_total,
            context_low,
            middle,
            ffn_rows,
            gate_pre,
            up_pre,
            product,
        ) = saved_state
        grad_low = grad_result.astype(jnp.bfloat16)
        grad_rows = lax.all_gather(grad_low, "tensor", axis=0, tiled=True)
        grad_w_down = outer_sum(product, grad_rows)
        grad_product = project_back(grad_rows, w_down)
        _, pull_ffn = jax.vjp(gated, gate_pre, up_pre)
        grad_gate, grad_up = pull_ffn(grad_product)
        grad_gate = grad_gate.astype(jnp.bfloat16)
        grad_up = grad_up.astype(jnp.bfloat16)
        grad_w_gate = outer_sum(ffn_rows, grad_gate)
        grad_w_up = outer_sum(ffn_rows, grad_up)
        grad_ffn_in = lax.psum_scatter(
            (project_back(grad_gate, w_gate) + project_back(grad_up, w_up)).astype(jnp.bfloat16),
            "tensor",
            scatter_dimension=0,
            tiled=True,
        ).astype(jnp.float32)
        _, pull_norm = jax.vjp(rms_norm, middle, ffn_gain)
        grad_middle_norm, grad_ffn_gain = pull_norm(grad_ffn_in)
        grad_middle = grad_result + grad_middle_norm
        grad_mid_low = grad_middle.astype(jnp.bfloat16)
        grad_w_out = outer_sum(context_low, grad_mid_low)
        grad_context = project_back(grad_mid_low, w_out).astype(jnp.bfloat16)
        grad_grp = grad_context.reshape(
            seq_count, half_len, KV_HEADS, group_size, HEAD_DIM
        ).transpose(2, 0, 3, 1, 4)
        grad_query, grad_key, grad_value = lax.map(
            attend_back, (query_grp, key_grp, value_grp, grad_grp, log_total)
        )
        key_terms = grad_key.transpose(1, 2, 0, 3).reshape(seq_count, -1, KV_HEADS * HEAD_DIM)
        value_terms = grad_value.transpose(1, 2, 0, 3).reshape(seq_count, -1, KV_HEADS * HEAD_DIM)
        key_sum, value_sum = (
            lax.psum_scatter(
                key_terms.astype(jnp.bfloat16), "tensor", scatter_dimension=1, tiled=True
            ).astype(jnp.float32),
            lax.psum_scatter(
                value_terms.astype(jnp.bfloat16), "tensor", scatter_dimension=1, tiled=True
            ).astype(jnp.float32),
        )
        grad_key_pre = rotate(
            key_sum.reshape(seq_count, half_len, KV_HEADS, HEAD_DIM), cos_table, -sin_table
        )
        grad_key_pre = grad_key_pre.astype(jnp.bfloat16).reshape(row_count, KV_HEADS * HEAD_DIM)
        grad_value_pre = value_sum.reshape(row_count, KV_HEADS * HEAD_DIM).astype(jnp.bfloat16)
        grad_query_all = grad_query.transpose(1, 3, 0, 2, 4).reshape(
            seq_count, half_len, HEADS, HEAD_DIM
        )
        grad_query_pre = (
            rotate(grad_query_all, cos_table, -sin_table)
            .astype(jnp.bfloat16)
            .reshape(row_count, model_width)
        )
        grad_w_query = outer_sum(normed, grad_query_pre)
        grad_w_key = outer_sum(normed, grad_key_pre)
        grad_w_value = outer_sum(normed, grad_value_pre)
        grad_normed = (
            project_back(grad_query_pre, w_query)
            + project_back(grad_key_pre, w_key)
            + project_back(grad_value_pre, w_value)
        )
        _, pull_attn = jax.vjp(rms_norm, stream, attn_gain)
        grad_stream_norm, grad_attn_gain = pull_attn(grad_normed)
        grad_terms = (
            grad_attn_gain,
            grad_w_query,
            grad_w_key,
            grad_w_value,
            grad_w_out,
            grad_ffn_gain,
            grad_w_gate,
            grad_w_up,
            grad_w_down,
        )
        return (grad_middle + grad_stream_norm, grad_terms)

    stream_in = tokens.reshape(row_count, model_width).astype(jnp.float32)
    first_out, _ = forward(stream_in)
    second_out, _ = forward(first_out)
    grad_first, terms_second = backward(
        first_out, cotangent.reshape(row_count, model_width).astype(jnp.float32)
    )
    grad_input, terms_first = backward(stream_in, grad_first)
    summed = reduce_end(
        tuple((left_sum + right_sum for left_sum, right_sum in zip(terms_second, terms_first)))
    )
    output = second_out.reshape(seq_count, half_len, model_width).astype(jnp.bfloat16)
    return (output, grad_input.reshape(seq_count, half_len, model_width)) + summed


def solution(mesh):
    in_specs = (
        P("dp", "tensor", None),
        P("dp", None),
        P("dp", "tensor", None),
        P(),
        P(),
        P(),
        P(),
        P(),
        P(),
        P(None, "tensor"),
        P(None, "tensor"),
        P("tensor", None),
    )
    out_specs = (
        P("dp", "tensor", None),
        P("dp", "tensor", None),
        P(),
        P(),
        P(),
        P(),
        P(),
        P(),
        P(None, "tensor"),
        P(None, "tensor"),
        P("tensor", None),
    )
    return jax.shard_map(
        per_device, mesh=mesh, in_specs=in_specs, out_specs=out_specs, check_vma=False
    )
```

profile of v0, /device:TPU:0, one launch (start us, length us, event | category | flops | bytes accessed | tf_op | source)
XLA Modules:
  0.0 781.1 jit_solution(8146894250012975624)
XLA Ops:
  19.6 33.2 %while.78 = (s32[]{:T(128)}, bf16[3,1,3,512,64]{3,4,2,1,0:T(8,128)(2,1)}, bf16[3,1,3,512,64]{3,4,2,1,0:T(8,128)(2,1)}, bf16[3,1,1024,64]{2,3,1,0:T(8,128)(2,1)},...) while((s32[]{:T(128)}, ...), condition=%wide.region_4.5_spmd.clone, body=%wide.region_1.4_spmd.clone.sunk | while | flops 413664256 | bytes 14510181 | solution.py:161
  20.1 6.0 fusion.438
  26.1 4.6 fusion.439
  31.2 5.9 fusion.438
  37.1 4.6 fusion.439
  42.2 5.9 fusion.438
  48.2 4.6 fusion.439
  56.6 11.9 %all-gather.10.cloned.1.call-done = bf16[1024,576]{0,1:T(8,128)(2,1)} async-done(((bf16[512,576]{0,1:T(8,128)(2,1)}), bf16[1024,576]{0,1:T(8,128)(2,1)}) %all-gather.10.cloned.1.call-update) | async-done | bytes 1179664 | tf_op jit(solution)/shard_map/all_gather | solution.py:167
  73.0 6.7 convolution_convert_fusion.1
  79.9 23.6 %while.82 = (s32[]{:T(128)}, bf16[3,1,3,512,64]{3,4,2,1,0:T(8,128)(2,1)S(1)}, f32[3,1,3,512]{3,2,1,0:T(4,128)S(1)}, bf16[3,1,3,512,64]{3,4,2,1,0:T(8,128)(2,1)},...) while((s32[]{:T(128)}, ...), condition=%wide.region_30.31_spmd.clone, body=%wide.region_27.30_spmd.clone.sunk | while | flops 423098880 | bytes 21897328 | solution.py:161
  115.0 23.5 %while.80 = (s32[]{:T(128)}, bf16[3,1,3,512,64]{3,4,2,1,0:T(8,128)(2,1)S(1)}, f32[3,1,3,512]{3,2,1,0:T(4,128)S(1)}, bf16[3,1,3,512,64]{3,4,2,1,0:T(8,128)(2,1)},...) while((s32[]{:T(128)}, ...), condition=%wide.region_17.18_spmd.clone, body=%wide.region_14.17_spmd.clone.sunk | while | flops 423098880 | bytes 21897328 | solution.py:161
  142.2 9.7 %all-gather.14.cloned.1.call-done = bf16[1024,576]{0,1:T(8,128)(2,1)} async-done(((bf16[512,576]{0,1:T(8,128)(2,1)}), bf16[1024,576]{0,1:T(8,128)(2,1)}) %all-gather.14.cloned.1.call-update) | async-done | bytes 1179664 | tf_op jit(solution)/shard_map/all_gather | solution.py:167
  151.9 4.8 fusion.300
  163.8 5.9 multiply_convert_fusion.5
  174.0 9.7 %reduce-scatter.13.cloned.1.call-done = bf16[512,576]{0,1:T(8,128)(2,1)} async-done(((bf16[1024,576]{0,1:T(8,128)(2,1)}), bf16[512,576]{0,1:T(8,128)(2,1)}) %reduce-scatter.13.cloned.1.call-update) | async-done | bytes 589840 | tf_op jit(solution)/shard_map/reduce_scatter | solution.py:214
  192.1 44.7 %while.81 = (s32[]{:T(128)}, f32[3,1,3,512,64]{3,4,2,1,0:T(8,128)}, bf16[3,1,1024,64]{2,3,1,0:T(8,128)(2,1)}, bf16[3,1,1024,64]{2,3,1,0:T(8,128)(2,1)}, bf16[3,1...) while((s32[]{:T(128)}, f32[3,1,3,512,64]{3,4,2,1,0:T(8,128)}, ...), condition=%wide.region_23.24_spmd.clone, body=%wide.region_21.23_spmd.clone.sunk | while | flops 1031961088 | bytes 56949980 | solution.py:229
  240.7 5.2 reduce-scatter.15.cloned.1.call-done
  250.1 7.7 reduce-scatter.17.cloned.1.call-done
  264.4 5.4 all-gather.18.cloned.1.call-done
  269.8 4.7 fusion.304
  277.6 4.8 all-gather.16.cloned.1.call-done
  282.3 5.9 multiply_convert_fusion.4
  292.5 34.3 %while.79 = (s32[]{:T(128)}, bf16[3,1,3,512,64]{3,4,2,1,0:T(8,128)(2,1)S(1)}, bf16[3,1,3,512,64]{3,4,2,1,0:T(8,128)(2,1)}, bf16[3,1,1024,64]{2,3,1,0:T(8,128)(2,...) while((s32[]{:T(128)}, ...), condition=%wide.region_11.12_spmd.clone, body=%wide.region_8.11_spmd.clone.sunk | while | flops 413664256 | bytes 14512229 | solution.py:161
  293.8 6.1 fusion.443
  305.3 6.1 fusion.443
  316.7 6.1 fusion.443
  328.6 5.4 fusion.204
  342.4 39.1 %while.83 = (s32[]{:T(128)}, f32[3,1,3,512,64]{3,4,2,1,0:T(8,128)}, bf16[3,1,1024,64]{2,3,1,0:T(8,128)(2,1)}, bf16[3,1,1024,64]{2,3,1,0:T(8,128)(2,1)}, bf16[3,1...) while((s32[]{:T(128)}, f32[3,1,3,512,64]{3,4,2,1,0:T(8,128)}, ...), condition=%wide.region_36.37_spmd.clone, body=%wide.region_34.36_spmd.clone.sunk | while | flops 1031961088 | bytes 54590656 | solution.py:229
  394.1 6.4 convolution_convert_fusion
  431.2 40.6 %all-reduce = (f32[576]{0:T(1024)}, f32[576]{0:T(1024)}) all-reduce(f32[576]{0:T(1024)S(1)} %add.317, f32[576]{0:T(1024)S(1)} %add.322), channel_id=1, replica_groups=mesh['dp'=16,'tensor'=2] {'dp','tensor'}, use_global_device_ids=true, to_apply=%region_42.43 | all-reduce | flops 1152 | bytes 9216 | tf_op jit(solution)/shard_map/psum | solution.py:57
  476.9 86.3 %all-reduce.6.cloned.1.call-done = (f32[576,576]{1,0:T(8,128)}, f32[576,192]{0,1:T(8,128)}, f32[576,192]{0,1:T(8,128)}, f32[576,576]{1,0:T(8,128)}) async-done(((f32[576,576]{1,0:T(8,128)}, f32[576,192]{0,1:T(8,128)}, f32[576,192]{0,1:T(8,128)}, f32[576,576]{1,0:T(8,128)}), (f32[576,576]{1,0:T(8,128)}, f32[576,192]{0,1:T(8,128)}, f32[576,192]{0,1:T(8,128)}, ...) | async-done | bytes 3538960 | tf_op jit(solution)/shard_map/psum | solution.py:57
  563.2 199.2 %all-reduce.8.cloned.1.call-done = (f32[576,768]{1,0:T(8,128)}, f32[576,768]{1,0:T(8,128)}, f32[768,576]{0,1:T(8,128)}) async-done(((f32[576,768]{1,0:T(8,128)}, f32[576,768]{1,0:T(8,128)}, f32[768,576]{0,1:T(8,128)}), (f32[576,768]{1,0:T(8,128)}, f32[576,768]{1,0:T(8,128)}, f32[768,576]{0,1:T(8,128)})) %all-reduce.8.cloned.1.call-update) | async-done | bytes 5308432 | tf_op jit(solution)/shard_map/psum | solution.py:61
  (467 shorter events, 294.5 us)
Async XLA Ops:
  7.2 61.4 %copy-start = (bf16[576,768]{1,0:T(8,128)(2,1)S(1)}, bf16[576,768]{1,0:T(8,128)(2,1)}, u32[]{:S(2)}) copy-start(bf16[576,768]{1,0:T(8,128)(2,1)} %param.33) | copy-start | bytes 2654212
  7.2 61.4 %all-gather.10.cloned.1.call-start = ((), (), s32[]{:S(2)}) async-start(), calls=%async_computation.8 | async-start | bytes 1769472 | tf_op jit(solution)/shard_map/all_gather | solution.py:167
  7.4 49.3 %copy-start.15 = (bf16[3,1,3,512,64]{3,4,2,1,0:T(8,128)(2,1)}, bf16[3,1,3,512,64]{3,4,2,1,0:T(8,128)(2,1)S(1)}, u32[]{:S(2)}) copy-start(bf16[3,1,3,512,64]{3,4,2,1,0:T(8,128)(2,1)S(1)} %fusion.296) | copy-start | bytes 1769476
  8.9 6.4 copy-start.75
  12.7 99.0 %copy-start.35 = (f32[512,32]{0,1:T(8,128)}, f32[512,32]{0,1:T(8,128)S(1)}, u32[]{:S(2)}) copy-start(f32[512,32]{0,1:T(8,128)S(1)} %get-tuple-element.626) | copy-start | bytes 196612
  19.6 33.2 %copy-start.5 = (bf16[576,576]{1,0:T(8,128)(2,1)S(1)}, bf16[576,576]{1,0:T(8,128)(2,1)}, u32[]{:S(2)}) copy-start(bf16[576,576]{1,0:T(8,128)(2,1)} %param.31) | copy-start | bytes 1990660
  56.6 48.7 %reduce-scatter.9.cloned.1.call-start = ((), (), s32[]{:S(2)}) async-start(), calls=%async_computation.9 | async-start | bytes 1769472 | tf_op jit(solution)/shard_map/reduce_scatter | solution.py:171
  73.0 7.0 copy-start.21
  79.7 72.2 %all-gather.14.cloned.1.call-start = ((), (), s32[]{:S(2)}) async-start(), calls=%async_computation.12 | async-start | bytes 1769472 | tf_op jit(solution)/shard_map/all_gather | solution.py:167
  105.2 34.1 %copy-start.85 = (f32[512]{0:T(512)}, f32[512]{0:T(512)S(1)}, u32[]{:S(2)}) copy-start(f32[512]{0:T(512)S(1)} %get-tuple-element.629) | copy-start | bytes 6148
  141.3 22.5 %all-gather.20.cloned.1.call-start = ((), (), s32[]{:S(2)}) async-start(), calls=%async_computation.21 | async-start | bytes 1769472 | tf_op jit(solution)/shard_map/all_gather | solution.py:205
  141.9 41.8 %reduce-scatter.13.cloned.1.call-start = ((), (), s32[]{:S(2)}) async-start(), calls=%async_computation.13 | async-start | bytes 1769472 | tf_op jit(solution)/shard_map/reduce_scatter | solution.py:214
  173.7 72.2 %reduce-scatter.15.cloned.1.call-start = ((), (), s32[]{:S(2)}) async-start(), calls=%async_computation.14 | async-start | bytes 589824 | tf_op jit(solution)/shard_map/reduce_scatter | solution.py:235
  192.1 46.3 %copy-start.36 = (f32[512,32]{0,1:T(8,128)S(1)}, f32[512,32]{0,1:T(8,128)}, u32[]{:S(2)}) copy-start(f32[512,32]{0,1:T(8,128)} %copy-done.35) | copy-start | bytes 196612
  192.1 46.3 %copy-start.55 = (f32[512,32]{0,1:T(8,128)S(1)}, f32[512,32]{0,1:T(8,128)}, u32[]{:S(2)}) copy-start(f32[512,32]{0,1:T(8,128)} %get-tuple-element.624) | copy-start | bytes 196612
  236.8 21.0 %reduce-scatter.17.cloned.1.call-start = ((), (), s32[]{:S(2)}) async-start(), calls=%async_computation.15 | async-start | bytes 589824 | tf_op jit(solution)/shard_map/reduce_scatter | solution.py:238
  237.5 32.2 %all-gather.18.cloned.1.call-start = ((), (), s32[]{:S(2)}) async-start(), calls=%async_computation.17 | async-start | bytes 1769472 | tf_op jit(solution)/shard_map/all_gather | solution.py:167
  238.3 44.0 %all-gather.16.cloned.1.call-start = ((), (), s32[]{:S(2)}) async-start(), calls=%async_computation.16 | async-start | bytes 1769472 | tf_op jit(solution)/shard_map/all_gather | solution.py:205
  247.7 11.6 %copy-start.24 = (bf16[576,576]{1,0:T(8,128)(2,1)S(1)}, bf16[576,576]{1,0:T(8,128)(2,1)}, u32[]{:S(2)}) copy-start(bf16[576,576]{1,0:T(8,128)(2,1)} %param.28) | copy-start | bytes 1990660
  263.9 70.1 %reduce-scatter.19.cloned.1.call-start = ((), (), s32[]{:S(2)}) async-start(), calls=%async_computation.18 | async-start | bytes 1769472 | tf_op jit(solution)/shard_map/reduce_scatter | solution.py:214
  292.2 97.4 %all-gather.12.cloned.1.call-start = ((), (), s32[]{:S(2)}) async-start(), calls=%async_computation.10 | async-start | bytes 1769472 | tf_op jit(solution)/shard_map/all_gather | solution.py:167
  328.6 5.4 copy-start.12
  328.6 5.4 copy-start.74
  328.6 5.4 copy-start.78
  339.4 69.3 %reduce-scatter.21.cloned.1.call-start = ((), (), s32[]{:S(2)}) async-start(), calls=%async_computation.19 | async-start | bytes 589824 | tf_op jit(solution)/shard_map/reduce_scatter | solution.py:235
  381.5 30.2 %reduce-scatter.23.cloned.1.call-start = ((), (), s32[]{:S(2)}) async-start(), calls=%async_computation.20 | async-start | bytes 589824 | tf_op jit(solution)/shard_map/reduce_scatter | solution.py:238
  389.3 85.2 %reduce-scatter.11.cloned.1.call-start = ((), (), s32[]{:S(2)}) async-start(), calls=%async_computation.11 | async-start | bytes 1769472 | tf_op jit(solution)/shard_map/reduce_scatter | solution.py:171
  394.1 6.5 copy-start.50
  400.5 162.7 %all-reduce.6.cloned.1.call-start = ((), (), s32[]{:S(2)}) async-start(), calls=%async_computation.22 | async-start | bytes 7864320 | tf_op jit(solution)/shard_map/psum | solution.py:57
  414.1 348.3 %all-reduce.8.cloned.1.call-start = ((), (), s32[]{:S(2)}) async-start(), calls=%async_computation.23 | async-start | bytes 10616832 | tf_op jit(solution)/shard_map/psum | solution.py:61
  429.3 42.5 %copy-start.82 = (f32[512]{0:T(512)S(1)}, f32[512]{0:T(512)}, u32[]{:S(2)}) copy-start(f32[512]{0:T(512)} %copy-done.81) | copy-start | bytes 6148
  563.2 201.9 %copy-start.65 = (f32[576,192]{0,1:T(8,128)S(1)}, f32[576,192]{0,1:T(8,128)}, u32[]{:S(2)}) copy-start(f32[576,192]{0,1:T(8,128)} %get-tuple-element.1267) | copy-start | bytes 1327108
  (101 other events, 217.7 us)
Sparse Core Ops, SparseCore 0:
  56.7 11.8 all-gather.9
  79.8 9.8 reduce-scatter.8
  141.4 10.3 all-gather.13
  153.3 10.3 all-gather.19
  173.8 9.8 reduce-scatter.12
  236.9 8.9 reduce-scatter.14
  248.8 8.9 reduce-scatter.16
  259.3 10.3 all-gather.17
  271.9 10.3 all-gather.15
  292.4 9.8 reduce-scatter.18
  339.5 10.3 all-gather.11
  381.6 8.9 reduce-scatter.20
  392.9 8.9 reduce-scatter.22
  404.0 9.8 reduce-scatter.10
  420.3 142.8 all-reduce.5
  571.2 191.1 all-reduce.7
where the time goes:
time: 791 us; the launch traced here: 781 us
  waiting for transfers between devices  346 us (44%)
  matrix products  266 us (34%)
  other arithmetic  61.8 us (8%)
  blocking collectives  49.6 us (6%)
  local copies, waits for them, and re-layouts  39.2 us (5%)
  between operations  15.6 us (2%)
    psum x1, waiting for transfers between devices, reduce_end(): column = lax.psum((grad_terms[6], grad_terms[7], grad_terms[8]), 'dp')  199 us
    psum x1, waiting for transfers between devices, reduce_end(): lax.psum((grad_terms[0], grad_terms[1], grad_terms[2], grad_terms[3], gra...  86.3 us
    dot_general x18, matrix products, project(): return jnp.dot(left_mat, right_mat, preferred_element_type=jnp.float32)  46.3 us
    dot_general x12, matrix products, attend_group(): jnp.einsum('srqk,skd->srqd', attn_probs, value_grp, preferred_element_typ...  44.6 us
    psum x1, blocking collectives, reduce_end(): lax.psum((grad_terms[0], grad_terms[1], grad_terms[2], grad_terms[3], gra...  40.6 us
    sub x6, matrix products, attend_group(): exp_scores = jnp.exp(scores - top_score)  36.3 us
    dot_general x14, matrix products, outer_sum(): jnp.einsum('rd,rf->df', left_mat, right_mat, preferred_element_type=jnp.f...  32.6 us
    dot_general x14, matrix products, project_back(): jnp.einsum('rf,df->rd', left_mat, right_mat, preferred_element_type=jnp.f...  30.9 us
  transfers between devices with their start and end apart: 16, of which 10 were waited for; matrix products, arithmetic and copies ran while one was open for 23% of the time, Pallas kernels for 0%

commit v1 on v0

v1 whole, which is shorter than its diff:
```python
import math

import jax
import jax.numpy as jnp
from jax import lax
from jax.experimental import pallas as pl
from jax.experimental.pallas import tpu as pltpu
from jax.sharding import PartitionSpec as P

HEADS = 9
KV_HEADS = 3
GROUP = HEADS // KV_HEADS
HEAD_DIM = 64
HALF = HEAD_DIM // 2
EPSILON = 1e-05
MASKED = -1e30
BLOCK = 256
SCALE = HEAD_DIM ** (-0.5)
F32 = jnp.float32
BF16 = jnp.bfloat16
VMEM_LIMIT = 50 * 2**20


def dot(left, right, left_dim, right_dim):
    return lax.dot_general(
        left, right, (((left_dim,), (right_dim,)), ((), ())), preferred_element_type=F32
    )


def pieces(size, step):
    return [slice(start, start + step) for start in range(0, size, step)]


def inverse_rms(x_ref):
    total = None
    for rows in pieces(x_ref.shape[0], 64):
        x = x_ref[rows, :]
        part = jnp.sum(x * x, axis=0, keepdims=True)
        total = part if total is None else total + part
    return lax.rsqrt(total / x_ref.shape[0] + EPSILON)


def norm_forward(x_ref, gain_ref, out_ref):
    scale = inverse_rms(x_ref)
    for rows in pieces(x_ref.shape[0], 64):
        out_ref[rows, :] = (x_ref[rows, :] * scale * gain_ref[rows, :]).astype(BF16)


def norm_backward(x_ref, gain_ref, grad_ref, add_ref, out_ref, gain_grad_ref):
    scale = inverse_rms(x_ref)
    inner = None
    for rows in pieces(x_ref.shape[0], 64):
        x, e = x_ref[rows, :], grad_ref[rows, :]
        xe = x * e
        gain_grad_ref[rows, :] = jnp.sum(xe * scale, axis=1, keepdims=True)
        part = jnp.sum(xe * gain_ref[rows, :], axis=0, keepdims=True)
        inner = part if inner is None else inner + part
    cubed = scale * scale * scale * (inner / x_ref.shape[0])
    for rows in pieces(x_ref.shape[0], 64):
        out_ref[rows, :] = (
            add_ref[rows, :].astype(F32)
            + scale * gain_ref[rows, :] * grad_ref[rows, :]
            - x_ref[rows, :] * cubed
        )


def rotated(x, cos_table, sin_table):
    front, back = x[:HALF], x[HALF:]
    return jnp.concatenate(
        [front * cos_table - back * sin_table, back * cos_table + front * sin_table], axis=0
    )


def project_qkv(normed_ref, wq_ref, wk_ref, wv_ref, cos_ref, sin_ref, q_ref, kv_ref):
    normed = normed_ref[...]
    cos_table, sin_table = cos_ref[...], sin_ref[...]
    key = dot(wk_ref[...], normed, 0, 0)
    for head in pieces(KV_HEADS * HEAD_DIM, HEAD_DIM):
        kv_ref[head, :] = rotated(key[head], cos_table, sin_table).astype(BF16)
    kv_ref[KV_HEADS * HEAD_DIM :, :] = dot(wv_ref[...], normed, 0, 0).astype(BF16)
    query = dot(wq_ref[...], normed, 0, 0)
    for head in pieces(HEADS * HEAD_DIM, HEAD_DIM):
        q_ref[head, :] = (rotated(query[head], cos_table, sin_table) * SCALE).astype(BF16)


def first_kernel(
    tokens_ref, gain_ref, wq_ref, wk_ref, wv_ref, cos_ref, sin_ref, x_ref, normed_ref, q_ref, kv_ref
):
    x_ref[...] = tokens_ref[...].astype(F32).T
    norm_forward(x_ref, gain_ref, normed_ref)
    project_qkv(normed_ref, wq_ref, wk_ref, wv_ref, cos_ref, sin_ref, q_ref, kv_ref)


def load_keys(core, own_ref, other_ref, all_ref, tok_ref):
    half = own_ref.shape[1]
    all_ref[core] = own_ref[...]
    all_ref[1 - core] = other_ref[...]
    for part in range(2):
        for head in range(2 * KV_HEADS):
            rows = slice(head * HEAD_DIM, (head + 1) * HEAD_DIM)
            tok_ref[head, part * half : (part + 1) * half, :] = all_ref[part, rows, :].T


def set_mask(bias_ref, place, kb, doc_start):
    key_place = kb * BLOCK + lax.broadcasted_iota(jnp.int32, (BLOCK, BLOCK), 0)
    bias_ref[...] = jnp.where((key_place >= doc_start) & (key_place <= place), 0.0, MASKED)


def attend_kernel(
    info_ref, start_ref, q_ref, own_ref, other_ref, ctx_ref, lse_ref,
    all_ref, tok_ref, bias_ref, m_ref, l_ref, acc_ref,
):
    core = info_ref[0]
    half = own_ref.shape[1]
    tiles = half // BLOCK
    load_keys(core, own_ref, other_ref, all_ref, tok_ref)
    for tile in range(tiles):
        cols = slice(tile * BLOCK, (tile + 1) * BLOCK)
        doc_start = start_ref[0:1, cols]
        place = core * half + tile * BLOCK + lax.broadcasted_iota(jnp.int32, (1, BLOCK), 1)
        m_ref[...] = jnp.full(m_ref.shape, MASKED, F32)
        l_ref[...] = jnp.zeros(l_ref.shape, F32)
        acc_ref[...] = jnp.zeros(acc_ref.shape, F32)

        def step(kb, carry):
            set_mask(bias_ref, place, kb, doc_start)
            part, inside = kb // tiles, kb % tiles
            keys = pl.ds(pl.multiple_of(kb * BLOCK, BLOCK), BLOCK)
            inner = pl.ds(pl.multiple_of(inside * BLOCK, BLOCK), BLOCK)
            for group in range(KV_HEADS):
                key = tok_ref[group, keys, :]
                value = all_ref[
                    part, (KV_HEADS + group) * HEAD_DIM : (KV_HEADS + group + 1) * HEAD_DIM, inner
                ]
                for head in range(group * GROUP, (group + 1) * GROUP):
                    rows = slice(head * HEAD_DIM, (head + 1) * HEAD_DIM)
                    scores = dot(key, q_ref[rows, cols], 1, 0) + bias_ref[...]
                    m_old = m_ref[head : head + 1, :]
                    m_new = jnp.maximum(m_old, jnp.max(scores, axis=0, keepdims=True))
                    probs = jnp.exp(scores - m_new)
                    fade = jnp.exp(m_old - m_new)
                    m_ref[head : head + 1, :] = m_new
                    l_ref[head : head + 1, :] = l_ref[head : head + 1, :] * fade + jnp.sum(
                        probs, axis=0, keepdims=True
                    )
                    acc_ref[rows, :] = acc_ref[rows, :] * fade + dot(
                        value, probs.astype(BF16), 1, 0
                    )
            return carry

        lax.fori_loop(info_ref[1 + tile], core * tiles + tile + 1, step, 0)
        for head in range(HEADS):
            rows = slice(head * HEAD_DIM, (head + 1) * HEAD_DIM)
            total = l_ref[head : head + 1, :]
            ctx_ref[rows, cols] = acc_ref[rows, :] * (1.0 / total)
            lse_ref[head : head + 1, cols] = m_ref[head : head + 1, :] + jnp.log(total)


def attend_back_kernel(
    info_ref, start_ref, q_ref, own_ref, other_ref, ctx_ref, lse_ref, grad_ref,
    dq_ref, dkv_own_ref, dkv_other_ref,
    all_ref, tok_ref, bias_ref, delta_ref, dkv_ref,
):
    core = info_ref[0]
    half = own_ref.shape[1]
    tiles = half // BLOCK
    load_keys(core, own_ref, other_ref, all_ref, tok_ref)
    dkv_ref[...] = jnp.zeros(dkv_ref.shape, F32)
    for head in range(HEADS):
        rows = slice(head * HEAD_DIM, (head + 1) * HEAD_DIM)
        delta_ref[head : head + 1, :] = jnp.sum(
            grad_ref[rows, :].astype(F32) * ctx_ref[rows, :], axis=0, keepdims=True
        )
    for tile in range(tiles):
        cols = slice(tile * BLOCK, (tile + 1) * BLOCK)
        doc_start = start_ref[0:1, cols]
        place = core * half + tile * BLOCK + lax.broadcasted_iota(jnp.int32, (1, BLOCK), 1)
        dq_ref[:, cols] = jnp.zeros((HEADS * HEAD_DIM, BLOCK), F32)

        def step(kb, carry):
            set_mask(bias_ref, place, kb, doc_start)
            part, inside = kb // tiles, kb % tiles
            keys = pl.ds(pl.multiple_of(kb * BLOCK, BLOCK), BLOCK)
            inner = pl.ds(pl.multiple_of(inside * BLOCK, BLOCK), BLOCK)
            for group in range(KV_HEADS):
                key = tok_ref[group, keys, :]
                value = tok_ref[KV_HEADS + group, keys, :]
                key_rows = slice(group * HEAD_DIM, (group + 1) * HEAD_DIM)
                value_rows = slice((KV_HEADS + group) * HEAD_DIM, (KV_HEADS + group + 1) * HEAD_DIM)
                key_cols = all_ref[part, key_rows, inner]
                dk = dkv_ref[part, key_rows, inner]
                dv = dkv_ref[part, value_rows, inner]
                for head in range(group * GROUP, (group + 1) * GROUP):
                    rows = slice(head * HEAD_DIM, (head + 1) * HEAD_DIM)
                    query = q_ref[rows, cols]
                    grad = grad_ref[rows, cols]
                    scores = dot(key, query, 1, 0) + bias_ref[...]
                    probs = jnp.exp(scores - lse_ref[head : head + 1, cols])
                    grad_probs = dot(value, grad, 1, 0)
                    grad_scores = (probs * (grad_probs - delta_ref[head : head + 1, cols])).astype(
                        BF16
                    )
                    dv = dv + dot(grad, probs.astype(BF16), 1, 1)
                    dk = dk + dot(query, grad_scores, 1, 1)
                    dq_ref[rows, cols] += dot(key_cols, grad_scores, 1, 0)
                dkv_ref[part, key_rows, inner] = dk
                dkv_ref[part, value_rows, inner] = dv
            return carry

        lax.fori_loop(info_ref[1 + tile], core * tiles + tile + 1, step, 0)
    dkv_own_ref[...] = dkv_ref[core]
    dkv_other_ref[...] = dkv_ref[1 - core].astype(BF16)


def attend_out(x_ref, ctx_ref, wo_ref, ctx_low_ref, mid_ref):
    ctx_low_ref[...] = ctx_ref[...].astype(BF16)
    mid_ref[...] = x_ref[...] + dot(wo_ref[...], ctx_low_ref[...], 0, 0)


def middle_kernel(
    x_ref, ctx_ref, wo_ref, ffn_gain_ref, wg_refs, wu_refs, wd_refs,
    gain_ref, wq_ref, wk_ref, wv_ref, cos_ref, sin_ref,
    ctx_low_ref, mid_ref, ffn_ref, x2_ref, normed_ref, q_ref, kv_ref,
):
    attend_out(x_ref, ctx_ref, wo_ref, ctx_low_ref, mid_ref)
    norm_forward(mid_ref, ffn_gain_ref, ffn_ref)
    ffn_in = ffn_ref[...]
    x2_ref[...] = mid_ref[...]
    for part in range(2):
        for hidden in pieces(wg_refs[part].shape[1], BLOCK):
            gate = dot(wg_refs[part][:, hidden], ffn_in, 0, 0)
            up = dot(wu_refs[part][:, hidden], ffn_in, 0, 0)
            product = (gate * jax.nn.sigmoid(gate) * up).astype(BF16)
            x2_ref[...] += dot(wd_refs[part][hidden, :], product, 0, 0)
    norm_forward(x2_ref, gain_ref, normed_ref)
    project_qkv(normed_ref, wq_ref, wk_ref, wv_ref, cos_ref, sin_ref, q_ref, kv_ref)


def ffn_terms(gate, up, grad_product):
    sig = jax.nn.sigmoid(gate)
    silu = gate * sig
    grad_gate = (grad_product * up * (sig + silu * (1.0 - sig))).astype(BF16)
    grad_up = (grad_product * silu).astype(BF16)
    return (silu * up).astype(BF16), grad_gate, grad_up


def out_back(grad_mid_ref, ctx_low_ref, wo_ref, low_ref, dwo_ref, grad_ctx_ref, earlier_ref):
    low_ref[...] = grad_mid_ref[...].astype(BF16)
    low = low_ref[...]
    term = dot(low, ctx_low_ref[...], 1, 1)
    dwo_ref[...] = term if earlier_ref is None else term + earlier_ref[...]
    grad_ctx_ref[...] = dot(wo_ref[...], low, 1, 0).astype(BF16)


def turn_kernel(
    x_ref, ctx_ref, wo_ref, ffn_gain_ref, wg_refs, wu_refs, wd_refs, cotangent_ref,
    output_ref, grad_low_ref, ffn_ref, prod_ref, gg_ref, gu_ref,
    grad_mid_ref, dwo_ref, grad_ctx_ref, dgain_ref,
    mid_ref, ctx_low_ref, acc_ref, low_ref,
):
    attend_out(x_ref, ctx_ref, wo_ref, ctx_low_ref, mid_ref)
    norm_forward(mid_ref, ffn_gain_ref, ffn_ref)
    ffn_in = ffn_ref[...]
    grad_low_ref[...] = cotangent_ref[...].T
    grad_low = grad_low_ref[...]
    half_hidden = wg_refs[0].shape[1]
    acc_ref[...] = mid_ref[...]
    grad_mid_ref[...] = jnp.zeros(grad_mid_ref.shape, F32)
    for part in range(2):
        for hidden in pieces(half_hidden, BLOCK):
            rows = slice(part * half_hidden + hidden.start, part * half_hidden + hidden.stop)
            gate = dot(wg_refs[part][:, hidden], ffn_in, 0, 0)
            up = dot(wu_refs[part][:, hidden], ffn_in, 0, 0)
            grad_product = dot(wd_refs[part][hidden, :], grad_low, 1, 0)
            product, grad_gate, grad_up = ffn_terms(gate, up, grad_product)
            prod_ref[rows, :] = product
            gg_ref[rows, :] = grad_gate
            gu_ref[rows, :] = grad_up
            acc_ref[...] += dot(wd_refs[part][hidden, :], product, 0, 0)
            grad_mid_ref[...] += dot(wg_refs[part][:, hidden], grad_gate, 1, 0) + dot(
                wu_refs[part][:, hidden], grad_up, 1, 0
            )
    output_ref[...] = acc_ref[...].T.astype(BF16)
    acc_ref[...] = grad_mid_ref[...]
    norm_backward(mid_ref, ffn_gain_ref, acc_ref, grad_low_ref, grad_mid_ref, dgain_ref)
    out_back(grad_mid_ref, ctx_low_ref, wo_ref, low_ref, dwo_ref, grad_ctx_ref, None)


def qkv_back(
    dq_ref, dkv_own_ref, dkv_got_ref, normed_ref, wq_ref, wk_ref, wv_ref, cos_ref, sin_ref,
    dpre_ref, dw_ref, dnormed_ref, earlier_ref,
):
    cos_table, sin_table = cos_ref[...], sin_ref[...]
    width, kv_width = HEADS * HEAD_DIM, KV_HEADS * HEAD_DIM
    for head in pieces(width, HEAD_DIM):
        dpre_ref[head, :] = rotated(dq_ref[head, :] * SCALE, cos_table, -sin_table).astype(BF16)
    for head in pieces(kv_width, HEAD_DIM):
        total = dkv_own_ref[head, :] + dkv_got_ref[head, :].astype(F32)
        rows = slice(width + head.start, width + head.stop)
        dpre_ref[rows, :] = rotated(total, cos_table, -sin_table).astype(BF16)
    dpre_ref[width + kv_width :, :] = (
        dkv_own_ref[kv_width:, :] + dkv_got_ref[kv_width:, :].astype(F32)
    ).astype(BF16)
    term = dot(dpre_ref[...], normed_ref[...], 1, 1)
    dw_ref[...] = term if earlier_ref is None else term + earlier_ref[...]
    dnormed_ref[...] = (
        dot(wq_ref[...], dpre_ref[:width, :], 1, 0)
        + dot(wk_ref[...], dpre_ref[width : width + kv_width, :], 1, 0)
        + dot(wv_ref[...], dpre_ref[width + kv_width :, :], 1, 0)
    )


def between_kernel(
    dq_ref, dkv_own_ref, dkv_got_ref, normed_ref, x_ref, grad_mid_ref,
    gain_ref, wq_ref, wk_ref, wv_ref, cos_ref, sin_ref,
    mid1_ref, ffn1_ref, ctx_low1_ref, wo_ref, ffn_gain_ref, wg_refs, wu_refs, wd_refs,
    ffn2_ref, low2_ref, prod2_ref, gg2_ref, gu2_ref, dwo2_ref,
    dwqkv_ref, dgain_ref, grad_mid1_ref, dwo_ref, grad_ctx_ref, dffn_gain_ref,
    dwg_refs, dwu_refs, dwd_refs,
    dpre_ref, dnormed_ref, gstream_ref, low_ref, acc_ref,
):
    qkv_back(
        dq_ref, dkv_own_ref, dkv_got_ref, normed_ref, wq_ref, wk_ref, wv_ref, cos_ref, sin_ref,
        dpre_ref, dwqkv_ref, dnormed_ref, None,
    )
    norm_backward(x_ref, gain_ref, dnormed_ref, grad_mid_ref, gstream_ref, dgain_ref)
    low_ref[...] = gstream_ref[...].astype(BF16)
    low = low_ref[...]
    ffn_in = ffn1_ref[...]
    half_hidden = wg_refs[0].shape[1]
    acc_ref[...] = jnp.zeros(acc_ref.shape, F32)
    for part in range(2):
        for hidden in pieces(half_hidden, BLOCK):
            rows = slice(part * half_hidden + hidden.start, part * half_hidden + hidden.stop)
            gate = dot(wg_refs[part][:, hidden], ffn_in, 0, 0)
            up = dot(wu_refs[part][:, hidden], ffn_in, 0, 0)
            grad_product = dot(wd_refs[part][hidden, :], low, 1, 0)
            product, grad_gate, grad_up = ffn_terms(gate, up, grad_product)
            acc_ref[...] += dot(wg_refs[part][:, hidden], grad_gate, 1, 0) + dot(
                wu_refs[part][:, hidden], grad_up, 1, 0
            )
            dwg_refs[part][:, hidden] = (
                dot(ffn_in, grad_gate, 1, 1) + dot(ffn2_ref[...], gg2_ref[rows, :], 1, 1)
            ).astype(BF16)
            dwu_refs[part][:, hidden] = (
                dot(ffn_in, grad_up, 1, 1) + dot(ffn2_ref[...], gu2_ref[rows, :], 1, 1)
            ).astype(BF16)
            dwd_refs[part][hidden, :] = (
                dot(product, low, 1, 1) + dot(prod2_ref[rows, :], low2_ref[...], 1, 1)
            ).astype(BF16)
    norm_backward(mid1_ref, ffn_gain_ref, acc_ref, gstream_ref, grad_mid1_ref, dffn_gain_ref)
    out_back(grad_mid1_ref, ctx_low1_ref, wo_ref, low_ref, dwo_ref, grad_ctx_ref, dwo2_ref)


def last_kernel(
    dq_ref, dkv_own_ref, dkv_got_ref, normed_ref, x_ref, grad_mid_ref,
    gain_ref, wq_ref, wk_ref, wv_ref, cos_ref, sin_ref, dwqkv2_ref,
    dwqkv_ref, dgain_ref, out_ref,
    dpre_ref, dnormed_ref, gstream_ref,
):
    qkv_back(
        dq_ref, dkv_own_ref, dkv_got_ref, normed_ref, wq_ref, wk_ref, wv_ref, cos_ref, sin_ref,
        dpre_ref, dwqkv_ref, dnormed_ref, dwqkv2_ref,
    )
    norm_backward(x_ref, gain_ref, dnormed_ref, grad_mid_ref, gstream_ref, dgain_ref)
    out_ref[...] = gstream_ref[...].T


def shape(dims, dtype):
    return jax.ShapeDtypeStruct(dims, dtype)


def run(kernel, args, outs, scratch=(), smem=0, name=None):
    leaves, tree = jax.tree.flatten(args)
    out_leaves, out_tree = jax.tree.flatten(outs)
    n_in, n_out = len(leaves), len(out_leaves)

    def body(*refs):
        ins = jax.tree.unflatten(tree, refs[:n_in])
        results = jax.tree.unflatten(out_tree, refs[n_in : n_in + n_out])
        kernel(*ins, *results, *refs[n_in + n_out :])

    in_specs = [
        pl.BlockSpec(memory_space=pltpu.SMEM if index < smem else pltpu.VMEM)
        for index in range(n_in)
    ]
    results = pl.pallas_call(
        body,
        out_shape=out_leaves,
        in_specs=in_specs,
        out_specs=[pl.BlockSpec(memory_space=pltpu.VMEM)] * n_out,
        scratch_shapes=list(scratch),
        compiler_params=pltpu.CompilerParams(vmem_limit_bytes=VMEM_LIMIT),
        name=name,
    )(*leaves)
    return jax.tree.unflatten(out_tree, results)


def swap(array):
    return lax.ppermute(array, "tensor", [(0, 1), (1, 0)])


def partners(sizes, bits):
    n, cores = sizes
    return [
        (place * cores + core, (place ^ (1 << bits[core])) * cores + core)
        for place in range(n)
        for core in range(cores)
    ]


def reduce_chunks(array, sizes, orders):
    n, cores = sizes
    steps = len(orders[0])
    if n != 1 << steps:
        return lax.psum(array.astype(F32), "dp").astype(BF16)
    place = lax.axis_index("dp")
    core = lax.axis_index("tensor")
    bits = [
        jnp.where(core == 0, (place >> orders[0][step]) & 1, (place >> orders[1][step]) & 1)
        for step in range(steps)
    ]
    perms = [partners(sizes, (orders[0][step], orders[1][step])) for step in range(steps)]
    rest = array.shape[1:]
    for step in range(steps):
        halves = array.reshape((2, -1) + rest)
        kept = lax.dynamic_index_in_dim(halves, bits[step], 0, keepdims=False)
        sent = lax.dynamic_index_in_dim(halves, 1 - bits[step], 0, keepdims=False)
        got = lax.ppermute(sent, ("dp", "tensor"), perms[step])
        array = (kept.astype(F32) + got.astype(F32)).astype(BF16)
    for step in reversed(range(steps)):
        got = lax.ppermute(array, ("dp", "tensor"), perms[step])
        array = jnp.where(
            bits[step] == 0, jnp.concatenate([array, got]), jnp.concatenate([got, array])
        )
    return array


def sum_small(array, sizes):
    n, _ = sizes
    array = array + swap(array)
    steps = int(math.log2(n))
    if n != 1 << steps:
        return lax.psum(array, "dp")
    for step in range(steps):
        array = array + lax.ppermute(array, "dp", [(i, i ^ (1 << step)) for i in range(n)])
    return array


def per_device(
    sizes, tokens, segments, cotangent, attn_gain, w_query, w_key, w_value, w_out, ffn_gain,
    w_gate, w_up, w_down,
):
    _, half, width = tokens.shape
    kv_width = KV_HEADS * HEAD_DIM
    hidden = w_gate.shape[1]
    core = lax.axis_index("tensor")
    offset = core * half
    tokens, cotangent = tokens[0], cotangent[0]
    segments = segments[0]

    place = (offset + jnp.arange(half)).astype(F32)
    inverse = 10000.0 ** (-2.0 * jnp.arange(HALF).astype(F32) / HEAD_DIM)
    angles = inverse[:, None] * place[None, :]
    tables = (jnp.cos(angles), jnp.sin(angles))
    own_labels = lax.dynamic_slice_in_dim(segments, offset, half, 0)
    doc_start = jnp.sum((segments[:, None] < own_labels[None, :]).astype(jnp.int32), axis=0)
    info = jnp.concatenate([core[None], doc_start[::BLOCK] // BLOCK]).astype(jnp.int32)
    doc_start = doc_start[None, :]

    gate_pair = (w_gate, swap(w_gate))
    up_pair = (w_up, swap(w_up))
    down_pair = (w_down, swap(w_down))
    gain_col, ffn_gain_col = attn_gain[:, None], ffn_gain[:, None]
    projections = (w_query, w_key, w_value)

    act = shape((width, half), F32)
    low = shape((width, half), BF16)
    kv = shape((2 * kv_width, half), BF16)
    wide = shape((2 * hidden, half), BF16)
    column = shape((width, 1), F32)
    key_scratch = [
        pltpu.VMEM((2, 2 * kv_width, half), BF16),
        pltpu.VMEM((2 * KV_HEADS, 2 * half, HEAD_DIM), BF16),
        pltpu.VMEM((BLOCK, BLOCK), F32),
    ]
    act_scratch = pltpu.VMEM((width, half), F32)
    low_scratch = pltpu.VMEM((width, half), BF16)

    def attend(query, kv_own, kv_other):
        return run(
            attend_kernel,
            (info, doc_start, query, kv_own, kv_other),
            (act, shape((16, half), F32)),
            key_scratch
            + [pltpu.VMEM((16, BLOCK), F32), pltpu.VMEM((16, BLOCK), F32),
               pltpu.VMEM((width, BLOCK), F32)],
            smem=1,
            name="attend",
        )

    def attend_back(query, kv_own, kv_other, ctx, lse, grad):
        return run(
            attend_back_kernel,
            (info, doc_start, query, kv_own, kv_other, ctx, lse, grad),
            (act, shape((2 * kv_width, half), F32), kv),
            key_scratch
            + [pltpu.VMEM((16, half), F32), pltpu.VMEM((2, 2 * kv_width, half), F32)],
            smem=1,
            name="attend_back",
        )

    x1, normed1, query1, kv1 = run(
        first_kernel, (tokens, gain_col) + projections + tables, (act, low, low, kv), name="first"
    )
    kv1_other = swap(kv1)
    ctx1, lse1 = attend(query1, kv1, kv1_other)
    ctx_low1, mid1, ffn1, x2, normed2, query2, kv2 = run(
        middle_kernel,
        (x1, ctx1, w_out, ffn_gain_col, gate_pair, up_pair, down_pair, gain_col)
        + projections + tables,
        (low, act, low, act, low, low, kv),
        name="middle",
    )
    kv2_other = swap(kv2)
    ctx2, lse2 = attend(query2, kv2, kv2_other)
    (
        output, grad_low2, ffn2, prod2, gg2, gu2, grad_mid2, dwo2, grad_ctx2, dffn_gain2,
    ) = run(
        turn_kernel,
        (x2, ctx2, w_out, ffn_gain_col, gate_pair, up_pair, down_pair, cotangent),
        (shape((half, width), BF16), low, low, wide, wide, wide, act,
         shape((width, width), F32), low, column),
        [act_scratch, low_scratch, act_scratch, low_scratch],
        name="turn",
    )
    dq2, dkv_own2, dkv_sent2 = attend_back(query2, kv2, kv2_other, ctx2, lse2, grad_ctx2)
    dkv_got2 = swap(dkv_sent2)
    half_in = shape((width, hidden), BF16)
    half_out = shape((hidden, width), BF16)
    qkv_scratch = [
        pltpu.VMEM((width + 2 * kv_width, half), BF16), act_scratch, act_scratch,
    ]
    dw_qkv_shape = shape((width + 2 * kv_width, width), F32)
    (
        dw_qkv2, dgain2, grad_mid1, dwo, grad_ctx1, dffn_gain1, dw_gate, dw_up, dw_down,
    ) = run(
        between_kernel,
        (dq2, dkv_own2, dkv_got2, normed2, x2, grad_mid2, gain_col) + projections + tables
        + (mid1, ffn1, ctx_low1, w_out, ffn_gain_col, gate_pair, up_pair, down_pair,
           ffn2, grad_low2, prod2, gg2, gu2, dwo2),
        (dw_qkv_shape, column, act, shape((width, width), F32), low, column,
         (half_in, half_in), (half_in, half_in), (half_out, half_out)),
        qkv_scratch + [low_scratch, act_scratch],
        name="between",
    )
    n = sizes[0]
    steps = int(math.log2(n))
    order_a = list(range(steps))
    order_b = [1, 0] + order_a[2:] if steps > 1 else order_a
    orders = (order_a, order_b)

    def to_chunks(array):
        return array.reshape((n, -1) + array.shape[1:])

    def pair_sum(pair):
        return (pair[0].astype(F32) + swap(pair[1]).astype(F32)).astype(BF16)

    gate_up = jnp.concatenate([pair_sum(dw_gate), pair_sum(dw_up)], axis=0)
    gate_up = reduce_chunks(to_chunks(gate_up), sizes, orders)
    gate_up = gate_up.reshape(2, width, hidden).astype(F32)
    down = reduce_chunks(to_chunks(pair_sum(dw_down)), sizes, orders)
    down = down.reshape(hidden, width).astype(F32)

    dq1, dkv_own1, dkv_sent1 = attend_back(query1, kv1, kv1_other, ctx1, lse1, grad_ctx1)
    dkv_got1 = swap(dkv_sent1)
    dw_qkv, dgain1, grad_input = run(
        last_kernel,
        (dq1, dkv_own1, dkv_got1, normed1, x1, grad_mid1, gain_col) + projections + tables
        + (dw_qkv2,),
        (dw_qkv_shape, column, shape((half, width), F32)),
        qkv_scratch,
        name="last",
    )
    packed = jnp.concatenate([dw_qkv, dwo], axis=0).astype(BF16)
    rows = packed.shape[0] // 2
    mine = lax.dynamic_slice_in_dim(packed, core * rows, rows, 0)
    theirs = lax.dynamic_slice_in_dim(packed, (1 - core) * rows, rows, 0)
    part = (mine.astype(F32) + swap(theirs).astype(F32)).astype(BF16)
    part = reduce_chunks(to_chunks(part), sizes, orders).reshape(rows, width)
    got = swap(part)
    packed = jnp.where(
        core == 0, jnp.concatenate([part, got]), jnp.concatenate([got, part])
    ).astype(F32).T
    gains = jnp.concatenate([dgain1 + dgain2, dffn_gain1 + dffn_gain2], axis=1).T
    gains = sum_small(gains, sizes)
    ends = (width, width + kv_width, width + 2 * kv_width)
    return (
        output[None],
        grad_input[None],
        gains[0],
        packed[:, : ends[0]],
        packed[:, ends[0] : ends[1]],
        packed[:, ends[1] : ends[2]],
        packed[:, ends[2] :],
        gains[1],
        gate_up[0],
        gate_up[1],
        down,
    )


def solution(mesh):
    sizes = (mesh.shape["dp"], mesh.shape["tensor"])

    def local(*args):
        return per_device(sizes, *args)

    split = P("dp", "tensor", None)
    in_specs = (
        split, P("dp", None), split, P(), P(), P(), P(), P(), P(),
        P(None, "tensor"), P(None, "tensor"), P("tensor", None),
    )
    out_specs = (
        split, split, P(), P(), P(), P(), P(), P(),
        P(None, "tensor"), P(None, "tensor"), P("tensor", None),
    )
    return jax.shard_map(
        local, mesh=mesh, in_specs=in_specs, out_specs=out_specs, check_vma=False
    )
```

time: 791 us -> 307 us (0.39)
  waiting for transfers between devices: 346 us -> 65.6 us
  matrix products: 266 us -> 0 us
  Pallas kernels: 0 us -> 97.5 us
  starting transfers between devices: 2.68 us -> 62.7 us
  blocking collectives: 49.6 us -> 0 us
  other arithmetic: 61.8 us -> 24.3 us
  between operations: 15.6 us -> 1.83 us
  local copies, waits for them, and re-layouts: 39.2 us -> 49.5 us
    psum x2 -> x0, waiting for transfers between devices: 286 us -> none  [the longest x1 199 us: reduce_end(): column = lax.psum((grad_terms[6], grad_terms[7], grad_terms[8]), 'dp')]
    dot_general x94 -> x0, matrix products: 229 us -> none  [the longest x18 46.3 us: project(): return jnp.dot(left_mat, right_mat, preferred_element_type=jnp.float32)]
    pallas_call x0 -> x9, Pallas kernels: none -> 97.5 us  [run(): pl.pallas_call(body, out_shape=out_leaves, in_specs=in_specs, out_specs=[...]
    ppermute x0 -> x41, waiting for transfers between devices: none -> 65.6 us  [the longest x12 33.5 us: reduce_chunks(): got = lax.ppermute(sent, ('dp', 'tensor'), perms[step])]
    ppermute x0 -> x41, starting transfers between devices: none -> 62.7 us  [the longest x4 25.9 us: sum_small(): lax.ppermute(array, 'dp', [(i, i ^ 1 << step) for i in range(n)])]
    psum x1 -> x0, blocking collectives: 40.6 us -> none  [reduce_end(): lax.psum((grad_terms[0], grad_terms[1], grad_terms[2], grad_terms[3], gra...]
    sub x6 -> x0, matrix products: 36.3 us -> none  [attend_group(): exp_scores = jnp.exp(scores - top_score)]
    all_gather x6 -> x0, waiting for transfers between devices: 35.8 us -> none  [the longest x4 27 us: forward(): ffn_rows = lax.all_gather(ffn_in, 'tensor', axis=0, tiled=True)]
  transfers between devices with their start and end apart: 16 -> 41, of which waited for: 10 -> 21; matrix products, arithmetic and copies ran while one was open for 23% -> 17% of each run, Pallas kernels for 0% -> 9%
where the time goes in v1:
time: 307 us; the launch traced here: 301 us
  Pallas kernels  97.5 us (32%)
  waiting for transfers between devices  65.6 us (21%)
  starting transfers between devices  62.7 us (20%)
  local copies, waits for them, and re-layouts  49.5 us (16%)
  other arithmetic  24.3 us (8%)
    pallas_call x9, Pallas kernels, run(): pl.pallas_call(body, out_shape=out_leaves, in_specs=in_specs, out_specs=[...  97.5 us
    ppermute x12, waiting for transfers between devices, reduce_chunks(): got = lax.ppermute(sent, ('dp', 'tensor'), perms[step])  33.5 us
    unnamed x100, local copies, waits for them, and re-layouts  29.3 us
    ppermute x4, starting transfers between devices, sum_small(): lax.ppermute(array, 'dp', [(i, i ^ 1 << step) for i in range(n)])  25.9 us
    ppermute x12, waiting for transfers between devices, reduce_chunks(): got = lax.ppermute(array, ('dp', 'tensor'), perms[step])  25.2 us
    ppermute x13, starting transfers between devices, swap(): return lax.ppermute(array, 'tensor', [(0, 1), (1, 0)])  22.6 us
    ppermute x12, starting transfers between devices, reduce_chunks(): got = lax.ppermute(array, ('dp', 'tensor'), perms[step])  8.54 us
    ppermute x4, local copies, waits for them, and re-layouts, swap(): return lax.ppermute(array, 'tensor', [(0, 1), (1, 0)])  7.52 us
  transfers between devices with their start and end apart: 41, of which 21 were waited for; matrix products, arithmetic and copies ran while one was open for 17% of the time, Pallas kernels for 9%

profile of v1, /device:TPU:0, one launch (start us, length us, event | category | flops | bytes accessed | tf_op | source)
XLA Modules:
  0.0 301.5 jit_solution(17735181501172623282)
XLA Ops:
  8.7 2.3 copy.109.refs_8_.refs_21_
  11.3 8.7 %attend.2 = (f32[576,512]{1,0:T(8,128)S(1)}, f32[16,512]{1,0:T(8,128)S(1)}) custom-call(s32[3]{0:T(128)S(1)} %pad_add_fusion.refs_0_, s32[1,512]{1,0:T(1,128)S(1)} %bitcast.79, bf16[576,512]{1,0:T(8,128)(2,1)S(1)} %get-tuple-element.58.refs_2_, bf16[384,512]{1,0:T(8,128)(2,1)S(1)} %get-tuple-element.59.refs_3_, bf16[384,512]{1,0:T(8,128)(2,1)S(1)} %collective-permute-done.refs_4_), custom_call_target="tpu_custom_call" | custom-call | tf_op jit(solution)/shard_map/attend/pallas_call | solution.py:387
  21.6 2.2 copy.110.refs_9_.refs_22_
  23.9 10.3 %middle.1 = (bf16[576,512]{1,0:T(8,128)(2,1)S(1)}, f32[576,512]{1,0:T(8,128)}, bf16[576,512]{1,0:T(8,128)(2,1)S(1)}, f32[576,512]{1,0:T(8,128)}, bf16[576,512]{1...) custom-call(f32[576,512]{1,0:T(8,128)} %get-tuple-element.57.refs_0_.refs_4_, ...), custom_call_target="tpu_custom_call" | custom-call | tf_op jit(solution)/shard_map/middle/pallas_call | solution.py:387
  36.6 5.3 %collective-permute-start.4 = (bf16[384,512]{1,0:T(8,128)(2,1)}, bf16[384,512]{1,0:T(8,128)(2,1)}, u32[]{:S(2)}, u32[]{:S(2)}) collective-permute-start(bf16[384,512]{1,0:T(8,128)(2,1)} %get-tuple-element.63.refs_3_), channel_id=1, source_target_pairs={{0,1},{1,0},{2,3},{3,2},{4,5},{5,4},{6,7},{7,6},{8,9},{9,8},{10,11... | collective-permute-start | bytes 1179656 | tf_op jit(solution)/shard_map/ppermute | solution.py:400
  43.6 9.5 %attend.3 = (f32[576,512]{1,0:T(8,128)S(1)}, f32[16,512]{1,0:T(8,128)S(1)}) custom-call(s32[3]{0:T(128)S(1)} %pad_add_fusion.refs_0_, s32[1,512]{1,0:T(1,128)S(1)} %bitcast.80, bf16[576,512]{1,0:T(8,128)(2,1)S(1)} %get-tuple-element.62.refs_2_, bf16[384,512]{1,0:T(8,128)(2,1)} %get-tuple-element.63.refs_3_, bf16[384,512]{1,0:T(8,128)(2,1)} %collective-permute-done.4.refs_4_), custom_call_target="tpu_custom_call" | custom-call | tf_op jit(solution)/shard_map/attend/pallas_call | solution.py:387
  54.1 14.6 %turn.1 = (bf16[512,576]{1,0:T(8,128)(2,1)S(1)}, bf16[576,512]{1,0:T(8,128)(2,1)S(1)}, bf16[576,512]{1,0:T(8,128)(2,1)S(1)}, bf16[1536,512]{1,0:T(8,128)(2,1)}, ...) custom-call(f32[576,512]{1,0:T(8,128)} %get-tuple-element.61.refs_0_, ...), custom_call_target="tpu_custom_call" | custom-call | tf_op jit(solution)/shard_map/turn/pallas_call | solution.py:387
  72.0 10.7 %attend_back.2 = (f32[576,512]{1,0:T(8,128)}, f32[384,512]{1,0:T(8,128)S(1)}, bf16[384,512]{1,0:T(8,128)(2,1)S(1)}) custom-call(s32[3]{0:T(128)S(1)} %pad_add_fusion.refs_0_, s32[1,512]{1,0:T(1,128)S(1)} %bitcast.81, bf16[576,512]{1,0:T(8,128)(2,1)S(1)} %get-tuple-element.62.refs_2_, bf16[384,512]{1,0:T(8,128)(2,1)} %get-tuple-element.63.refs_3_, ...), custom_call_target="tpu_custom_call" | custom-call | tf_op jit(solution)/shard_map/attend_back/pallas_call | solution.py:387
  83.6 9.9 %collective-permute-start.5 = (bf16[384,512]{1,0:T(8,128)(2,1)S(1)}, bf16[384,512]{1,0:T(8,128)(2,1)S(1)}, u32[]{:S(2)}, u32[]{:S(2)}) collective-permute-start(bf16[384,512]{1,0:T(8,128)(2,1)S(1)} %get-tuple-element.71), channel_id=1, source_target_pairs={{0,1},{1,0},{2,3},{3,2},{4,5},{5,4},{6,7},{7,6},{8,9},{9,8},{10,11... | collective-permute-start | bytes 1179656 | tf_op jit(solution)/shard_map/ppermute | solution.py:400
  94.8 24.5 %between.1 = (f32[960,576]{1,0:T(8,128)}, f32[576,1]{1,0:T(8,128)S(1)}, f32[576,512]{1,0:T(8,128)}, f32[576,576]{1,0:T(8,128)}, bf16[576,512]{1,0:T(8,128)(2,1)S...) custom-call(f32[576,512]{1,0:T(8,128)} %get-tuple-element.69.refs_0_, ...), custom_call_target="tpu_custom_call" | custom-call | tf_op jit(solution)/shard_map/between/pallas_call | solution.py:387
  121.6 2.3 copy.134
  124.3 10.4 %attend_back.3 = (f32[576,512]{1,0:T(8,128)}, f32[384,512]{1,0:T(8,128)S(1)}, bf16[384,512]{1,0:T(8,128)(2,1)}) custom-call(s32[3]{0:T(128)S(1)} %pad_add_fusion.refs_0_, s32[1,512]{1,0:T(1,128)S(1)} %bitcast.82, bf16[576,512]{1,0:T(8,128)(2,1)S(1)} %get-tuple-element.58.refs_2_, bf16[384,512]{1,0:T(8,128)(2,1)S(1)} %copy-done.8, ...), custom_call_target="tpu_custom_call" | custom-call | tf_op jit(solution)/shard_map/attend_back/pallas_call | solution.py:387
  135.5 4.9 %collective-permute-start.6 = (bf16[384,512]{1,0:T(8,128)(2,1)}, bf16[384,512]{1,0:T(8,128)(2,1)S(1)}, u32[]{:S(2)}, u32[]{:S(2)}) collective-permute-start(bf16[384,512]{1,0:T(8,128)(2,1)} %get-tuple-element.86), channel_id=1, source_target_pairs={{0,1},{1,0},{2,3},{3,2},{4,5},{5,4},{6,7},{7,6},{8,9},{9,8},{10,11... | collective-permute-start | bytes 1179656 | tf_op jit(solution)/shard_map/ppermute | solution.py:400
  143.3 2.3 convert.18
  146.2 6.9 %last.1 = (f32[960,576]{1,0:T(8,128)}, f32[576,1]{1,0:T(8,128)S(1)}, f32[512,576]{1,0:T(8,128)}) custom-call(f32[576,512]{1,0:T(8,128)} %get-tuple-element.84.refs_0_, f32[384,512]{1,0:T(8,128)S(1)} %copy-done.13, bf16[384,512]{1,0:T(8,128)(2,1)S(1)} %collective-permute-done.6.refs_2_, bf16[576,512]{1,0:T(8,128)(2,1)S(1)} %copy-done.17, ...), custom_call_target="tpu_custom_call" | custom-call | tf_op jit(solution)/shard_map/last/pallas_call | solution.py:387
  158.7 21.7 %collective-permute-start.8 = (f32[2,576]{1,0:T(2,128)S(1)}, f32[2,576]{1,0:T(2,128)S(1)}, u32[]{:S(2)}, u32[]{:S(2)}) collective-permute-start(f32[2,576]{1,0:T(2,128)S(1)} %fusion.12), channel_id=1, source_target_pairs={{0,2},{2,0},{4,6},{6,4},{8,10},{10,8},{12,14},{14,12},{16,18},{18,... | collective-permute-start | bytes 13832 | tf_op jit(solution)/shard_map/ppermute | solution.py:446
  186.0 2.2 copy.130
  188.2 3.0 collective-permute-done.33
  194.2 7.3 %collective-permute-done.34 = bf16[4,48,576]{2,1,0:T(8,128)(2,1)S(1)} collective-permute-done((bf16[4,48,576]{2,1,0:T(8,128)(2,1)S(1)}, bf16[4,48,576]{2,1,0:T(8,128)(2,1)S(1)}, u32[]{:S(2)}, u32[]{:S(2)}) %collective-permute-start.34) | collective-permute-done | bytes 221216 | tf_op jit(solution)/shard_map/ppermute | solution.py:429
  203.3 3.8 %collective-permute-done.35 = bf16[2,48,576]{2,1,0:T(8,128)(2,1)S(1)} collective-permute-done((bf16[2,48,576]{2,1,0:T(8,128)(2,1)S(1)}, bf16[2,48,576]{2,1,0:T(8,128)(2,1)S(1)}, u32[]{:S(2)}, u32[]{:S(2)}) %collective-permute-start.35) | collective-permute-done | bytes 110624 | tf_op jit(solution)/shard_map/ppermute | solution.py:429
  207.5 4.8 %collective-permute-done.36 = bf16[1,48,576]{2,1,0:T(8,128)(2,1)S(1)} collective-permute-done((bf16[1,48,576]{2,1,0:T(8,128)(2,1)S(1)}, bf16[1,48,576]{2,1,0:T(8,128)(2,1)S(1)}, u32[]{:S(2)}, u32[]{:S(2)}) %collective-permute-start.36) | collective-permute-done | bytes 55328 | tf_op jit(solution)/shard_map/ppermute | solution.py:429
  212.5 3.4 %collective-permute-done.14 = bf16[4,48,576]{2,1,0:T(8,128)(2,1)S(1)} collective-permute-done((bf16[4,48,576]{2,1,0:T(8,128)(2,1)S(1)}, bf16[4,48,576]{2,1,0:T(8,128)(2,1)S(1)}, u32[]{:S(2)}, u32[]{:S(2)}) %collective-permute-start.14) | collective-permute-done | bytes 221216 | tf_op jit(solution)/shard_map/ppermute | solution.py:429
  217.7 3.9 %collective-permute-done.15 = bf16[2,48,576]{2,1,0:T(8,128)(2,1)S(1)} collective-permute-done((bf16[2,48,576]{2,1,0:T(8,128)(2,1)S(1)}, bf16[2,48,576]{2,1,0:T(8,128)(2,1)S(1)}, u32[]{:S(2)}, u32[]{:S(2)}) %collective-permute-start.15) | collective-permute-done | bytes 110624 | tf_op jit(solution)/shard_map/ppermute | solution.py:429
  222.2 4.6 %collective-permute-done.16 = bf16[1,48,576]{2,1,0:T(8,128)(2,1)S(1)} collective-permute-done((bf16[1,48,576]{2,1,0:T(8,128)(2,1)S(1)}, bf16[1,48,576]{2,1,0:T(8,128)(2,1)S(1)}, u32[]{:S(2)}, u32[]{:S(2)}) %collective-permute-start.16) | collective-permute-done | bytes 55328 | tf_op jit(solution)/shard_map/ppermute | solution.py:429
  227.8 4.4 %collective-permute-done.17 = bf16[1,48,576]{2,1,0:T(8,128)(2,1)S(1)} collective-permute-done((bf16[1,48,576]{2,1,0:T(8,128)(2,1)S(1)}, bf16[1,48,576]{2,1,0:T(8,128)(2,1)S(1)}, u32[]{:S(2)}, u32[]{:S(2)}) %collective-permute-start.17) | collective-permute-done | bytes 55328 | tf_op jit(solution)/shard_map/ppermute | solution.py:432
  235.6 2.7 collective-permute-done.18
  241.7 7.0 %collective-permute-done.19 = bf16[4,48,576]{2,1,0:T(8,128)(2,1)S(1)} collective-permute-done((bf16[4,48,576]{2,1,0:T(8,128)(2,1)S(1)}, bf16[4,48,576]{2,1,0:T(8,128)(2,1)S(1)}, u32[]{:S(2)}, u32[]{:S(2)}) %collective-permute-start.19) | collective-permute-done | bytes 221216 | tf_op jit(solution)/shard_map/ppermute | solution.py:432
  252.2 4.7 %collective-permute-done.28 = bf16[1,72,768]{2,1,0:T(8,128)(2,1)S(1)} collective-permute-done((bf16[1,72,768]{2,1,0:T(8,128)(2,1)S(1)}, bf16[1,72,768]{2,1,0:T(8,128)(2,1)S(1)}, u32[]{:S(2)}, u32[]{:S(2)}) %collective-permute-start.28) | collective-permute-done | bytes 110624 | tf_op jit(solution)/shard_map/ppermute | solution.py:432
  260.5 2.5 collective-permute-done.9
  277.7 3.3 %collective-permute-done.30 = bf16[4,72,768]{2,1,0:T(8,128)(2,1)} collective-permute-done((bf16[4,72,768]{2,1,0:T(8,128)(2,1)S(1)}, bf16[4,72,768]{2,1,0:T(8,128)(2,1)}, u32[]{:S(2)}, u32[]{:S(2)}) %collective-permute-start.30) | collective-permute-done | bytes 442400 | tf_op jit(solution)/shard_map/ppermute | solution.py:432
  293.7 2.9 collective-permute-done.31
  296.6 2.4 fusion
  (236 shorter events, 90.4 us)
Async XLA Ops:
  0.7 23.2 %collective-permute-start.1 = (bf16[576,768]{1,0:T(8,128)(2,1)}, bf16[576,768]{1,0:T(8,128)(2,1)}, u32[]{:S(2)}, u32[]{:S(2)}) collective-permute-start(bf16[576,768]{1,0:T(8,128)(2,1)} %refs_17_.1), channel_id=1, source_target_pairs={{0,1},{1,0},{2,3},{3,2},{4,5},{5,4},{6,7},{7,6},{8,9},{9,8},{10,11... | collective-permute-start | bytes 2654216 | tf_op jit(solution)/shard_map/ppermute | solution.py:400
  1.2 22.7 %collective-permute-start.2 = (bf16[576,768]{1,0:T(8,128)(2,1)}, bf16[576,768]{1,0:T(8,128)(2,1)}, u32[]{:S(2)}, u32[]{:S(2)}) collective-permute-start(bf16[576,768]{1,0:T(8,128)(2,1)} %refs_19_.1), channel_id=1, source_target_pairs={{0,1},{1,0},{2,3},{3,2},{4,5},{5,4},{6,7},{7,6},{8,9},{9,8},{10,11... | collective-permute-start | bytes 2654216 | tf_op jit(solution)/shard_map/ppermute | solution.py:400
  1.3 20.4 %collective-permute-start.3 = (bf16[768,576]{0,1:T(8,128)(2,1)}, bf16[768,576]{0,1:T(8,128)(2,1)}, u32[]{:S(2)}, u32[]{:S(2)}) collective-permute-start(bf16[768,576]{0,1:T(8,128)(2,1)} %param.23), channel_id=1, source_target_pairs={{0,1},{1,0},{2,3},{3,2},{4,5},{5,4},{6,7},{7,6},{8,9},{9,8},{10,11... | collective-permute-start | bytes 2654216 | tf_op jit(solution)/shard_map/ppermute | solution.py:400
  36.6 7.0 %collective-permute-start.4 = (bf16[384,512]{1,0:T(8,128)(2,1)}, bf16[384,512]{1,0:T(8,128)(2,1)}, u32[]{:S(2)}, u32[]{:S(2)}) collective-permute-start(bf16[384,512]{1,0:T(8,128)(2,1)} %get-tuple-element.63.refs_3_), channel_id=1, source_target_pairs={{0,1},{1,0},{2,3},{3,2},{4,5},{5,4},{6,7},{7,6},{8,9},{9,8},{10,11... | collective-permute-start | bytes 1179656 | tf_op jit(solution)/shard_map/ppermute | solution.py:400
  83.6 11.3 %collective-permute-start.5 = (bf16[384,512]{1,0:T(8,128)(2,1)S(1)}, bf16[384,512]{1,0:T(8,128)(2,1)S(1)}, u32[]{:S(2)}, u32[]{:S(2)}) collective-permute-start(bf16[384,512]{1,0:T(8,128)(2,1)S(1)} %get-tuple-element.71), channel_id=1, source_target_pairs={{0,1},{1,0},{2,3},{3,2},{4,5},{5,4},{6,7},{7,6},{8,9},{9,8},{10,11... | collective-permute-start | bytes 1179656 | tf_op jit(solution)/shard_map/ppermute | solution.py:400
  123.9 56.4 %collective-permute-start.32 = (bf16[768,576]{0,1:T(8,128)(2,1)}, bf16[768,576]{0,1:T(8,128)(2,1)}, u32[]{:S(2)}, u32[]{:S(2)}) collective-permute-start(bf16[768,576]{0,1:T(8,128)(2,1)} %copy.134), channel_id=1, source_target_pairs={{0,1},{1,0},{2,3},{3,2},{4,5},{5,4},{6,7},{7,6},{8,9},{9,8},{10,11... | collective-permute-start | bytes 2654216 | tf_op jit(solution)/shard_map/ppermute | solution.py:400
  135.5 10.6 %collective-permute-start.6 = (bf16[384,512]{1,0:T(8,128)(2,1)}, bf16[384,512]{1,0:T(8,128)(2,1)S(1)}, u32[]{:S(2)}, u32[]{:S(2)}) collective-permute-start(bf16[384,512]{1,0:T(8,128)(2,1)} %get-tuple-element.86), channel_id=1, source_target_pairs={{0,1},{1,0},{2,3},{3,2},{4,5},{5,4},{6,7},{7,6},{8,9},{9,8},{10,11... | collective-permute-start | bytes 1179656 | tf_op jit(solution)/shard_map/ppermute | solution.py:400
  145.6 36.7 %collective-permute-start.23 = (bf16[576,768]{1,0:T(8,128)(2,1)}, bf16[576,768]{1,0:T(8,128)(2,1)}, u32[]{:S(2)}, u32[]{:S(2)}) collective-permute-start(bf16[576,768]{1,0:T(8,128)(2,1)} %get-tuple-element.100), channel_id=1, source_target_pairs={{0,1},{1,0},{2,3},{3,2},{4,5},{5,4},{6,7},{7,6},{8,9},{9,8},{10,11... | collective-permute-start | bytes 2654216 | tf_op jit(solution)/shard_map/ppermute | solution.py:400
  145.8 38.7 %collective-permute-start.22 = (bf16[576,768]{1,0:T(8,128)(2,1)}, bf16[576,768]{1,0:T(8,128)(2,1)}, u32[]{:S(2)}, u32[]{:S(2)}) collective-permute-start(bf16[576,768]{1,0:T(8,128)(2,1)} %get-tuple-element.98), channel_id=1, source_target_pairs={{0,1},{1,0},{2,3},{3,2},{4,5},{5,4},{6,7},{7,6},{8,9},{9,8},{10,11... | collective-permute-start | bytes 2654216 | tf_op jit(solution)/shard_map/ppermute | solution.py:400
  158.3 27.7 %collective-permute-start.12 = (bf16[768,576]{0,1:T(8,128)(2,1)}, bf16[768,576]{0,1:T(8,128)(2,1)}, u32[]{:S(2)}, u32[]{:S(2)}) collective-permute-start(bf16[768,576]{0,1:T(8,128)(2,1)} %copy.129), channel_id=1, source_target_pairs={{0,1},{1,0},{2,3},{3,2},{4,5},{5,4},{6,7},{7,6},{8,9},{9,8},{10,11... | collective-permute-start | bytes 2654216 | tf_op jit(solution)/shard_map/ppermute | solution.py:400
  158.7 100.7 %collective-permute-start.8 = (f32[2,576]{1,0:T(2,128)S(1)}, f32[2,576]{1,0:T(2,128)S(1)}, u32[]{:S(2)}, u32[]{:S(2)}) collective-permute-start(f32[2,576]{1,0:T(2,128)S(1)} %fusion.12), channel_id=1, source_target_pairs={{0,2},{2,0},{4,6},{6,4},{8,10},{10,8},{12,14},{14,12},{16,18},{18,... | collective-permute-start | bytes 13832 | tf_op jit(solution)/shard_map/ppermute | solution.py:446
  182.2 9.0 %collective-permute-start.33 = (bf16[8,48,576]{2,1,0:T(8,128)(2,1)S(1)}, bf16[8,48,576]{2,1,0:T(8,128)(2,1)}, u32[]{:S(2)}, u32[]{:S(2)}) collective-permute-start(bf16[8,48,576]{2,1,0:T(8,128)(2,1)S(1)} %dynamic-slice_bitcast_fusion.1), channel_id=1, source_target_pairs={{0,2},{1,5},{2,0},{3,7},{4,6},{5,1},{6,4},{7,3},{8,10},{9,13},{10,... | collective-permute-start | bytes 1327112 | tf_op jit(solution)/shard_map/ppermute | solution.py:429
  192.5 8.9 %collective-permute-start.34 = (bf16[4,48,576]{2,1,0:T(8,128)(2,1)S(1)}, bf16[4,48,576]{2,1,0:T(8,128)(2,1)S(1)}, u32[]{:S(2)}, u32[]{:S(2)}) collective-permute-start(bf16[4,48,576]{2,1,0:T(8,128)(2,1)S(1)} %dynamic-slice_bitcast_fusion.4), channel_id=1, source_target_pairs={{0,4},{1,3},{2,6},{3,1},{4,0},{5,7},{6,2},{7,5},{8,12},{9,11},{10,... | collective-permute-start | bytes 663560 | tf_op jit(solution)/shard_map/ppermute | solution.py:429
  194.1 13.2 %collective-permute-start.13 = (bf16[8,48,576]{2,1,0:T(8,128)(2,1)S(1)}, bf16[8,48,576]{2,1,0:T(8,128)(2,1)S(1)}, u32[]{:S(2)}, u32[]{:S(2)}) collective-permute-start(bf16[8,48,576]{2,1,0:T(8,128)(2,1)S(1)} %dynamic-slice_bitcast_fusion.2), channel_id=1, source_target_pairs={{0,2},{1,5},{2,0},{3,7},{4,6},{5,1},{6,4},{7,3},{8,10},{9,13},{10,... | collective-permute-start | bytes 1327112 | tf_op jit(solution)/shard_map/ppermute | solution.py:429
  201.7 15.7 %collective-permute-start.24 = (bf16[8,72,768]{2,1,0:T(8,128)(2,1)S(1)}, bf16[8,72,768]{2,1,0:T(8,128)(2,1)S(1)}, u32[]{:S(2)}, u32[]{:S(2)}) collective-permute-start(bf16[8,72,768]{2,1,0:T(8,128)(2,1)S(1)} %dynamic-slice_bitcast_fusion), channel_id=1, source_target_pairs={{0,2},{1,5},{2,0},{3,7},{4,6},{5,1},{6,4},{7,3},{8,10},{9,13},{10,... | collective-permute-start | bytes 2654216 | tf_op jit(solution)/shard_map/ppermute | solution.py:429
  207.4 8.4 %collective-permute-start.14 = (bf16[4,48,576]{2,1,0:T(8,128)(2,1)S(1)}, bf16[4,48,576]{2,1,0:T(8,128)(2,1)S(1)}, u32[]{:S(2)}, u32[]{:S(2)}) collective-permute-start(bf16[4,48,576]{2,1,0:T(8,128)(2,1)S(1)} %dynamic-slice_bitcast_fusion.5), channel_id=1, source_target_pairs={{0,4},{1,3},{2,6},{3,1},{4,0},{5,7},{6,2},{7,5},{8,12},{9,11},{10,... | collective-permute-start | bytes 663560 | tf_op jit(solution)/shard_map/ppermute | solution.py:429
  212.4 14.9 %collective-permute-start.37 = (bf16[1,48,576]{2,1,0:T(8,128)(2,1)S(1)}, bf16[1,48,576]{2,1,0:T(8,128)(2,1)S(1)}, u32[]{:S(2)}, u32[]{:S(2)}) collective-permute-start(bf16[1,48,576]{2,1,0:T(8,128)(2,1)S(1)} %add_convert_fusion.5), channel_id=1, source_target_pairs={{0,16},{1,17},{2,18},{3,19},{4,20},{5,21},{6,22},{7,23},{8,24},{9,... | collective-permute-start | bytes 165896 | tf_op jit(solution)/shard_map/ppermute | solution.py:432
  216.0 5.6 %collective-permute-start.15 = (bf16[2,48,576]{2,1,0:T(8,128)(2,1)S(1)}, bf16[2,48,576]{2,1,0:T(8,128)(2,1)S(1)}, u32[]{:S(2)}, u32[]{:S(2)}) collective-permute-start(bf16[2,48,576]{2,1,0:T(8,128)(2,1)S(1)} %dynamic-slice_bitcast_fusion.8), channel_id=1, source_target_pairs={{0,8},{1,9},{2,10},{3,11},{4,12},{5,13},{6,14},{7,15},{8,0},{9,1},... | collective-permute-start | bytes 331784 | tf_op jit(solution)/shard_map/ppermute | solution.py:429
  222.1 10.2 %collective-permute-start.25 = (bf16[4,72,768]{2,1,0:T(8,128)(2,1)S(1)}, bf16[4,72,768]{2,1,0:T(8,128)(2,1)S(1)}, u32[]{:S(2)}, u32[]{:S(2)}) collective-permute-start(bf16[4,72,768]{2,1,0:T(8,128)(2,1)S(1)} %dynamic-slice_bitcast_fusion.3), channel_id=1, source_target_pairs={{0,4},{1,3},{2,6},{3,1},{4,0},{5,7},{6,2},{7,5},{8,12},{9,11},{10,... | collective-permute-start | bytes 1327112 | tf_op jit(solution)/shard_map/ppermute | solution.py:429
  227.3 7.3 %collective-permute-start.38 = (bf16[2,48,576]{2,1,0:T(8,128)(2,1)S(1)}, bf16[2,48,576]{2,1,0:T(8,128)(2,1)S(1)}, u32[]{:S(2)}, u32[]{:S(2)}) collective-permute-start(bf16[2,48,576]{2,1,0:T(8,128)(2,1)S(1)} %maximum_select_fusion.12), channel_id=1, source_target_pairs={{0,8},{1,9},{2,10},{3,11},{4,12},{5,13},{6,14},{7,15},{8,0},{9,1},... | collective-permute-start | bytes 331784 | tf_op jit(solution)/shard_map/ppermute | solution.py:432
  232.2 6.0 %collective-permute-start.18 = (bf16[2,48,576]{2,1,0:T(8,128)(2,1)S(1)}, bf16[2,48,576]{2,1,0:T(8,128)(2,1)S(1)}, u32[]{:S(2)}, u32[]{:S(2)}) collective-permute-start(bf16[2,48,576]{2,1,0:T(8,128)(2,1)S(1)} %maximum_select_fusion.11), channel_id=1, source_target_pairs={{0,8},{1,9},{2,10},{3,11},{4,12},{5,13},{6,14},{7,15},{8,0},{9,1},... | collective-permute-start | bytes 331784 | tf_op jit(solution)/shard_map/ppermute | solution.py:432
  232.5 8.2 %collective-permute-start.26 = (bf16[2,72,768]{2,1,0:T(8,128)(2,1)S(1)}, bf16[2,72,768]{2,1,0:T(8,128)(2,1)S(1)}, u32[]{:S(2)}, u32[]{:S(2)}) collective-permute-start(bf16[2,72,768]{2,1,0:T(8,128)(2,1)S(1)} %dynamic-slice_bitcast_fusion.6), channel_id=1, source_target_pairs={{0,8},{1,9},{2,10},{3,11},{4,12},{5,13},{6,14},{7,15},{8,0},{9,1},... | collective-permute-start | bytes 663560 | tf_op jit(solution)/shard_map/ppermute | solution.py:429
  234.6 15.7 %collective-permute-start.39 = (bf16[4,48,576]{2,1,0:T(8,128)(2,1)S(1)}, bf16[4,48,576]{2,1,0:T(8,128)(2,1)S(1)}, u32[]{:S(2)}, u32[]{:S(2)}) collective-permute-start(bf16[4,48,576]{2,1,0:T(8,128)(2,1)S(1)} %maximum_select_fusion.9), channel_id=1, source_target_pairs={{0,4},{1,3},{2,6},{3,1},{4,0},{5,7},{6,2},{7,5},{8,12},{9,11},{10,... | collective-permute-start | bytes 663560 | tf_op jit(solution)/shard_map/ppermute | solution.py:432
  238.3 10.4 %collective-permute-start.19 = (bf16[4,48,576]{2,1,0:T(8,128)(2,1)S(1)}, bf16[4,48,576]{2,1,0:T(8,128)(2,1)S(1)}, u32[]{:S(2)}, u32[]{:S(2)}) collective-permute-start(bf16[4,48,576]{2,1,0:T(8,128)(2,1)S(1)} %maximum_select_fusion.8), channel_id=1, source_target_pairs={{0,4},{1,3},{2,6},{3,1},{4,0},{5,7},{6,2},{7,5},{8,12},{9,11},{10,... | collective-permute-start | bytes 663560 | tf_op jit(solution)/shard_map/ppermute | solution.py:432
  240.8 9.4 %collective-permute-start.27 = (bf16[1,72,768]{2,1,0:T(8,128)(2,1)S(1)}, bf16[1,72,768]{2,1,0:T(8,128)(2,1)S(1)}, u32[]{:S(2)}, u32[]{:S(2)}) collective-permute-start(bf16[1,72,768]{2,1,0:T(8,128)(2,1)S(1)} %constant_dynamic-slice_fusion.1), channel_id=1, source_target_pairs={{0,16},{1,17},{2,18},{3,19},{4,20},{5,21},{6,22},{7,23},{8,24},{9,... | collective-permute-start | bytes 331784 | tf_op jit(solution)/shard_map/ppermute | solution.py:429
  248.9 8.9 %collective-permute-start.20 = (bf16[8,48,576]{2,1,0:T(8,128)(2,1)S(1)}, bf16[8,48,576]{2,1,0:T(8,128)(2,1)S(1)}, u32[]{:S(2)}, u32[]{:S(2)}) collective-permute-start(bf16[8,48,576]{2,1,0:T(8,128)(2,1)S(1)} %maximum_select_fusion.5), channel_id=1, source_target_pairs={{0,2},{1,5},{2,0},{3,7},{4,6},{5,1},{6,4},{7,3},{8,10},{9,13},{10,... | collective-permute-start | bytes 1327112 | tf_op jit(solution)/shard_map/ppermute | solution.py:432
  250.2 6.6 %collective-permute-start.28 = (bf16[1,72,768]{2,1,0:T(8,128)(2,1)S(1)}, bf16[1,72,768]{2,1,0:T(8,128)(2,1)S(1)}, u32[]{:S(2)}, u32[]{:S(2)}) collective-permute-start(bf16[1,72,768]{2,1,0:T(8,128)(2,1)S(1)} %add_convert_fusion.4), channel_id=1, source_target_pairs={{0,16},{1,17},{2,18},{3,19},{4,20},{5,21},{6,22},{7,23},{8,24},{9,... | collective-permute-start | bytes 331784 | tf_op jit(solution)/shard_map/ppermute | solution.py:432
  250.4 23.9 %collective-permute-start.40 = (bf16[8,48,576]{2,1,0:T(8,128)(2,1)S(1)}, bf16[8,48,576]{2,1,0:T(8,128)(2,1)}, u32[]{:S(2)}, u32[]{:S(2)}) collective-permute-start(bf16[8,48,576]{2,1,0:T(8,128)(2,1)S(1)} %maximum_select_fusion.6), channel_id=1, source_target_pairs={{0,2},{1,5},{2,0},{3,7},{4,6},{5,1},{6,4},{7,3},{8,10},{9,13},{10,... | collective-permute-start | bytes 1327112 | tf_op jit(solution)/shard_map/ppermute | solution.py:432
  257.5 13.6 %collective-permute-start.29 = (bf16[2,72,768]{2,1,0:T(8,128)(2,1)}, bf16[2,72,768]{2,1,0:T(8,128)(2,1)}, u32[]{:S(2)}, u32[]{:S(2)}) collective-permute-start(bf16[2,72,768]{2,1,0:T(8,128)(2,1)} %maximum_select_fusion.10), channel_id=1, source_target_pairs={{0,8},{1,9},{2,10},{3,11},{4,12},{5,13},{6,14},{7,15},{8,0},{9,1},... | collective-permute-start | bytes 663560 | tf_op jit(solution)/shard_map/ppermute | solution.py:432
  259.3 25.1 %collective-permute-start.21 = (bf16[768,576]{0,1:T(8,128)(2,1)}, bf16[768,576]{0,1:T(8,128)(2,1)}, u32[]{:S(2)}, u32[]{:S(2)}) collective-permute-start(bf16[768,576]{0,1:T(8,128)(2,1)} %copy.131), channel_id=1, source_target_pairs={{0,1},{1,0},{2,3},{3,2},{4,5},{5,4},{6,7},{7,6},{8,9},{9,8},{10,11... | collective-permute-start | bytes 2654216 | tf_op jit(solution)/shard_map/ppermute | solution.py:400
  272.5 8.5 %collective-permute-start.30 = (bf16[4,72,768]{2,1,0:T(8,128)(2,1)S(1)}, bf16[4,72,768]{2,1,0:T(8,128)(2,1)}, u32[]{:S(2)}, u32[]{:S(2)}) collective-permute-start(bf16[4,72,768]{2,1,0:T(8,128)(2,1)S(1)} %maximum_select_fusion.7), channel_id=1, source_target_pairs={{0,4},{1,3},{2,6},{3,1},{4,0},{5,7},{6,2},{7,5},{8,12},{9,11},{10,... | collective-permute-start | bytes 1327112 | tf_op jit(solution)/shard_map/ppermute | solution.py:432
  283.2 13.4 %collective-permute-start.31 = (bf16[8,72,768]{2,1,0:T(8,128)(2,1)}, bf16[8,72,768]{2,1,0:T(8,128)(2,1)}, u32[]{:S(2)}, u32[]{:S(2)}) collective-permute-start(bf16[8,72,768]{2,1,0:T(8,128)(2,1)} %maximum_select_fusion.4), channel_id=1, source_target_pairs={{0,2},{1,5},{2,0},{3,7},{4,6},{5,1},{6,4},{7,3},{8,10},{9,13},{10,... | collective-permute-start | bytes 2654216 | tf_op jit(solution)/shard_map/ppermute | solution.py:432
  (54 other events, 293.9 us)
